TPU v7x, 128 devices: a whole 4x4x4 slice. The times are simulated.
128 devices in a mesh: lat: 32 (over y, x, core), lev: 4 (over z).
Axes of the slice: x: 4, y: 4, z: 4, core: 2. Of those that a mesh axis runs over, the one named last changes fastest.
Arguments:
- control: float32 [4, 32, 768, 1536], P(None, 'lev', 'lat'), may hold values from -0.3 to 0.3
- obs_values: float32 [262144, 128], P(('lat', 'lev')), may hold values from -12 to 20
- obs_owner: int32 [262144, 1], P(('lat', 'lev')), may hold values from 0 to 127; in each aligned block of 2048 rows (0 to 2047, 2048 to 4095, ...) at most 32 rows name the same one
- obs_column: int32 [262144], P(('lat', 'lev')), may hold values from 0 to 9215
- sigma: float32 [4, 32, 768], replicated, may hold values from 0.5 to 2
- len_lon: float32 [4, 32], P(None, 'lev'), may hold values from 1.5 to 300
- len_lat: float32 [4, 32], P(None, 'lev'), may hold values from 1.5 to 150
- len_lev: float32 [4, 768], replicated, may hold values from 0.7 to 8
Outputs:
- gradient: float32 [4, 32, 768, 1536], P(None, 'lev', 'lat')
Inputs may be any that keep to these rules, and one draw needn't show every extreme that they name: `obs_owner`: the rows of one device name one owner at most 32 times; in every draw some device names some owner exactly 32 times.
All inputs are finite; a program needn't handle non-finite values.
Results may differ from a plain program's by a relative error of at most 0.0003.
Values sent between devices are 32-bit elements; how exact they have to be, the bound alone decides.
No kernel may reach another device: no remote copies, remote signals or barrier semaphores. Data moves between devices by JAX's collectives and lax.ppermute only.
A program may use at most 128 MiB of HBM per device.

v0:
```python
import jax
import jax.numpy as jnp
from jax import lax
from jax.sharding import PartitionSpec as P

F = 4
NLEV = 32
NLAT = 768
NLON = 1536
BLK = 128


precise_mode = lax.Precision.HIGHEST


def tri_matrix(scale, size):
    index_range = jnp.arange(size, dtype=jnp.int32)
    offset = (index_range[:, None] - index_range[None, :]).astype(jnp.float32)
    length = scale[..., None, None]
    decay = jnp.exp(-1.0 / length)
    return jnp.where(offset >= 0, (1.0 - decay) * jnp.exp(-jnp.maximum(offset, 0.0) / length), 0.0)


def carry_matrix(scale, blocks, periodic):
    index_range = jnp.arange(blocks, dtype=jnp.int32)
    offset = index_range[:, None] - 1 - index_range[None, :]
    length = scale[..., None, None]
    if periodic:
        spans = (offset % blocks).astype(jnp.float32) * BLK
        return jnp.exp(-spans / length) / (1.0 - jnp.exp(-(blocks * BLK) / length))
    spans = jnp.maximum(offset, 0).astype(jnp.float32) * BLK
    return jnp.where(offset >= 0, jnp.exp(-spans / length), 0.0)


def one_sweep(field, scale, axis, periodic, backward):
    shape = field.shape
    blocks = shape[axis] // BLK
    within = tri_matrix(scale, BLK)
    across = carry_matrix(scale, blocks, periodic)
    steps_in = (jnp.arange(BLK, dtype=jnp.int32) + 1).astype(jnp.float32)
    ramp = jnp.exp(-steps_in / scale[..., None])
    edge = BLK - 1
    if backward:
        within = jnp.swapaxes(within, 2, 3)
        across = jnp.swapaxes(across, 2, 3)
        ramp = ramp[..., ::-1]
        edge = 0
    if axis == 3:
        blocked = field.reshape(shape[0], shape[1], shape[2], blocks, BLK)
        local = jnp.einsum("flpbk,flik->flpbi", blocked, within, precision=precise_mode)
        carry = jnp.einsum("flpc,flbc->flpb", local[..., edge], across, precision=precise_mode)
        result = local + carry[..., None] * ramp[:, :, None, None, :]
    else:
        blocked = field.reshape(shape[0], shape[1], blocks, BLK, shape[3])
        local = jnp.einsum("flbkq,flik->flbiq", blocked, within, precision=precise_mode)
        carry = jnp.einsum(
            "flcq,flbc->flbq", local[:, :, :, edge, :], across, precision=precise_mode
        )
        result = local + carry[:, :, :, None, :] * ramp[:, :, None, :, None]
    return result.reshape(shape)


def smooth(field, scale, axis, periodic):
    return one_sweep(one_sweep(field, scale, axis, periodic, False), scale, axis, periodic, True)


def level_filter(field, scale):
    lower = tri_matrix(scale, field.shape[1])
    once = jnp.einsum("fkao,faik->fiao", field, lower, precision=precise_mode)
    return jnp.einsum("fkao,faki->fiao", once, lower, precision=precise_mode)


def bucket_slots(target, count_targets, capacity):
    onehot = (target[:, None] == jnp.arange(count_targets, dtype=jnp.int32)[None, :]).astype(
        jnp.float32
    )
    row_range = jnp.arange(target.shape[0], dtype=jnp.int32)
    earlier = (row_range[:, None] > row_range[None, :]).astype(jnp.float32)
    before = jnp.dot(earlier, onehot, precision=precise_mode)
    rank = jnp.sum(before * onehot, axis=1).astype(jnp.int32)
    return target * capacity + rank


def place_rows(values, slots, total_slots):
    slot_range = jnp.arange(total_slots, dtype=jnp.int32)
    placement = (slot_range[:, None] == slots[None, :]).astype(jnp.float32)
    return jnp.dot(placement, values, precision=precise_mode)


def place_ids(ids, slots, total_slots):
    slot_range = jnp.arange(total_slots, dtype=jnp.int32)
    return jnp.sum(jnp.where(slot_range[:, None] == slots[None, :], ids[None, :], 0), axis=1)


def spread_columns(values, ids, total):
    width = total
    while width > 2048 and width % 2 == 0:
        width = width // 2
    count_blocks = total // width
    values_t = jnp.transpose(values)

    def one_block(block_index):
        columns = block_index * width + jnp.arange(width, dtype=jnp.int32)
        hits = (ids[:, None] == columns[None, :]).astype(jnp.float32)
        return jnp.dot(values_t, hits, precision=precise_mode)

    stacked = lax.map(one_block, jnp.arange(count_blocks, dtype=jnp.int32))
    return jnp.transpose(stacked, (1, 0, 2)).reshape(values.shape[1], total)


def per_device(control, obs_values, obs_owner, obs_column, sigma, len_lon, len_lat, len_lev):
    n_lat = lax.axis_size("lat")
    n_lev = lax.axis_size("lev")
    devices = n_lat * n_lev
    row_count = obs_values.shape[0]
    capacity = 2 * row_count // devices
    lat_own = NLAT // n_lev
    lon_own = NLON // n_lat
    owner = obs_owner[:, 0]
    slots = bucket_slots(owner, devices, capacity)
    outgoing = place_rows(obs_values, slots, devices * capacity).reshape(
        devices * capacity, F, NLEV
    )
    targets = place_ids(obs_column, slots, devices * capacity)
    arrived, arrived_ids = (
        lax.all_to_all(outgoing, ("lat", "lev"), split_axis=0, concat_axis=0, tiled=True),
        lax.all_to_all(targets, ("lat", "lev"), split_axis=0, concat_axis=0, tiled=True),
    )
    flat_rows = arrived.reshape(-1, F * NLEV)
    columns = spread_columns(flat_rows, arrived_ids, lat_own * lon_own)
    columns = columns.reshape(F, NLEV, lat_own, lon_own)
    start = lax.axis_index("lev") * lat_own
    weights = lax.dynamic_slice_in_dim(sigma, start, lat_own, 2)
    own_scale = lax.dynamic_slice_in_dim(len_lev, start, lat_own, 1)
    columns = level_filter(columns * weights[:, :, :, None], own_scale)
    field = lax.all_to_all(columns, "lev", split_axis=1, concat_axis=2, tiled=True)
    field = smooth(field, len_lat, 2, False)
    field = lax.all_to_all(field, "lat", split_axis=2, concat_axis=3, tiled=True)
    field = smooth(field, len_lon, 3, True)
    return control + field


def solution(mesh):
    placed = (
        P(None, "lev", "lat", None),
        P(("lat", "lev"), None),
        P(("lat", "lev"), None),
        P(("lat", "lev")),
        P(),
        P(None, "lev"),
        P(None, "lev"),
        P(),
    )
    return jax.shard_map(
        per_device,
        mesh=mesh,
        in_specs=placed,
        out_specs=P(None, "lev", "lat", None),
        check_vma=False,
    )
```

profile of v0, /device:TPU:1, one launch (start us, length us, event | category | flops | bytes accessed | tf_op | source)
XLA Modules:
  0.0 618.5 jit_solution(11614436574148373337)
XLA Ops:
  6.9 11.7 %all-to-all-start = ((s32[128,32,1]{1,2,0:T(1,128)}), s32[128,32,1]{1,2,0:T(1,128)S(1)}, u32[]{:S(2)}, u32[]{:S(2)}) async-start(s32[128,32,1]{1,2,0:T(1,128)} %bitcast.4), calls=%async_computation | async-start | bytes 131072 | tf_op jit(solution)/shard_map/all_to_all | solution.py:127
  18.6 18.4 %fusion.5 = f32[4096,128]{0,1:T(8,128)S(1)} fusion(f32[2048,128]{1,0:T(8,128)S(1)} %copy-done, s32[2048]{0:T(1024)S(1)} %convert_add_fusion), kind=kOutput, calls=%fused_computation.9 | convolution fusion | flops 12893290496 | bytes 3153920 | tf_op jit(solution)/shard_map/dot_general | solution.py:87
  42.9 8.7 %reshape.188 = f32[128,1,4096]{2,1,0:T(1,128)} reshape(f32[4096,4,32]{2,1,0:T(4,128)} %copy.94) | data formatting | bytes 4194304
  51.6 9.8 %all-to-all-start.1 = ((f32[128,1,4096]{2,1,0:T(1,128)}), f32[128,1,4096]{2,1,0:T(1,128)S(1)}, u32[]{:S(2)}, u32[]{:S(2)}) async-start(f32[128,1,4096]{2,1,0:T(1,128)} %reshape.188), calls=%async_computation.1 | async-start | bytes 4194304 | tf_op jit(solution)/shard_map/all_to_all | solution.py:126
  64.8 27.2 %all-to-all-done.1 = f32[128,1,4096]{2,1,0:T(1,128)S(1)} async-done(((f32[128,1,4096]{2,1,0:T(1,128)}), f32[128,1,4096]{2,1,0:T(1,128)S(1)}, u32[]{:S(2)}, u32[]{:S(2)}) %all-to-all-start.1) | async-done | bytes 2097184 | tf_op jit(solution)/shard_map/all_to_all | solution.py:126
  93.8 7.2 %reduce.4 = f32[128,4096]{1,0:T(8,128)S(1)} reduce(f32[128,1,4096]{2,1,0:T(1,128)} %copy-done.3, f32[]{:T(128)} %broadcast.205), dimensions={1}, to_apply=%all_to_all.36.reduce_sub_computation | reduce | bytes 4194308 | tf_op jit(solution)/shard_map/all_to_all | solution.py:126
  113.7 105.1 %while.10 = (s32[]{:T(128)}, f32[8,128,1152]{1,2,0:T(8,128)}, s32[4096]{0:T(1024)S(1)}, s32[8]{0:T(128)S(1)}, f32[128,4096]{1,0:T(8,128)S(1)}, /*index=5*/s32[]{:T(128)}, s32[1]{0:T(128)}) while((s32[]{:T(128)}, f32[8,128,1152]{1,2,0:T(8,128)}, s32[4096]{0:T(1024)S(1)}, s32[8]{0:T(128)S(1)}, f32[128,4096]{1,0:T(8,128)S(1)}, ...), condition=%wide.region_3.4_spmd, body=%wide.region_2.3_spmd.sunk | while | flops 7257195520 | bytes 2713193 | solution.py:107
  115.6 11.7 %fusion.116 = f32[8,128,1152]{1,2,0:T(8,128)} fusion(f32[8,128,1152]{1,2,0:T(8,128)} %get-tuple-element.88, s32[]{:T(128)} %get-tuple-element.87, f32[128,4096]{1,0:T(8,128)S(1)} %get-tuple-element.98, s32[1152]{0:T(1024)S(1)} %iota_add_fusion.4, s32[4096]{0:T(1024)S(1)} %get-tuple-element.96), kind=kOutput, calls=%fused_computation.5.clone.1 | convolution fusion | flops 7257194496 | bytes 2708480 | tf_op jit(solution)/shard_map/while/body/eval_jaxpr/dot_general | solution.py:105
  128.6 11.7 %fusion.116 = f32[8,128,1152]{1,2,0:T(8,128)} fusion(f32[8,128,1152]{1,2,0:T(8,128)} %get-tuple-element.88, s32[]{:T(128)} %get-tuple-element.87, f32[128,4096]{1,0:T(8,128)S(1)} %get-tuple-element.98, s32[1152]{0:T(1024)S(1)} %iota_add_fusion.4, s32[4096]{0:T(1024)S(1)} %get-tuple-element.96), kind=kOutput, calls=%fused_computation.5.clone.1 | convolution fusion | flops 7257194496 | bytes 2708480 | tf_op jit(solution)/shard_map/while/body/eval_jaxpr/dot_general | solution.py:105
  141.7 11.7 %fusion.116 = f32[8,128,1152]{1,2,0:T(8,128)} fusion(f32[8,128,1152]{1,2,0:T(8,128)} %get-tuple-element.88, s32[]{:T(128)} %get-tuple-element.87, f32[128,4096]{1,0:T(8,128)S(1)} %get-tuple-element.98, s32[1152]{0:T(1024)S(1)} %iota_add_fusion.4, s32[4096]{0:T(1024)S(1)} %get-tuple-element.96), kind=kOutput, calls=%fused_computation.5.clone.1 | convolution fusion | flops 7257194496 | bytes 2708480 | tf_op jit(solution)/shard_map/while/body/eval_jaxpr/dot_general | solution.py:105
  154.8 11.7 %fusion.116 = f32[8,128,1152]{1,2,0:T(8,128)} fusion(f32[8,128,1152]{1,2,0:T(8,128)} %get-tuple-element.88, s32[]{:T(128)} %get-tuple-element.87, f32[128,4096]{1,0:T(8,128)S(1)} %get-tuple-element.98, s32[1152]{0:T(1024)S(1)} %iota_add_fusion.4, s32[4096]{0:T(1024)S(1)} %get-tuple-element.96), kind=kOutput, calls=%fused_computation.5.clone.1 | convolution fusion | flops 7257194496 | bytes 2708480 | tf_op jit(solution)/shard_map/while/body/eval_jaxpr/dot_general | solution.py:105
  167.9 11.7 %fusion.116 = f32[8,128,1152]{1,2,0:T(8,128)} fusion(f32[8,128,1152]{1,2,0:T(8,128)} %get-tuple-element.88, s32[]{:T(128)} %get-tuple-element.87, f32[128,4096]{1,0:T(8,128)S(1)} %get-tuple-element.98, s32[1152]{0:T(1024)S(1)} %iota_add_fusion.4, s32[4096]{0:T(1024)S(1)} %get-tuple-element.96), kind=kOutput, calls=%fused_computation.5.clone.1 | convolution fusion | flops 7257194496 | bytes 2708480 | tf_op jit(solution)/shard_map/while/body/eval_jaxpr/dot_general | solution.py:105
  181.0 11.7 %fusion.116 = f32[8,128,1152]{1,2,0:T(8,128)} fusion(f32[8,128,1152]{1,2,0:T(8,128)} %get-tuple-element.88, s32[]{:T(128)} %get-tuple-element.87, f32[128,4096]{1,0:T(8,128)S(1)} %get-tuple-element.98, s32[1152]{0:T(1024)S(1)} %iota_add_fusion.4, s32[4096]{0:T(1024)S(1)} %get-tuple-element.96), kind=kOutput, calls=%fused_computation.5.clone.1 | convolution fusion | flops 7257194496 | bytes 2708480 | tf_op jit(solution)/shard_map/while/body/eval_jaxpr/dot_general | solution.py:105
  194.0 11.7 %fusion.116 = f32[8,128,1152]{1,2,0:T(8,128)} fusion(f32[8,128,1152]{1,2,0:T(8,128)} %get-tuple-element.88, s32[]{:T(128)} %get-tuple-element.87, f32[128,4096]{1,0:T(8,128)S(1)} %get-tuple-element.98, s32[1152]{0:T(1024)S(1)} %iota_add_fusion.4, s32[4096]{0:T(1024)S(1)} %get-tuple-element.96), kind=kOutput, calls=%fused_computation.5.clone.1 | convolution fusion | flops 7257194496 | bytes 2708480 | tf_op jit(solution)/shard_map/while/body/eval_jaxpr/dot_general | solution.py:105
  207.1 11.7 %fusion.116 = f32[8,128,1152]{1,2,0:T(8,128)} fusion(f32[8,128,1152]{1,2,0:T(8,128)} %get-tuple-element.88, s32[]{:T(128)} %get-tuple-element.87, f32[128,4096]{1,0:T(8,128)S(1)} %get-tuple-element.98, s32[1152]{0:T(1024)S(1)} %iota_add_fusion.4, s32[4096]{0:T(1024)S(1)} %get-tuple-element.96), kind=kOutput, calls=%fused_computation.5.clone.1 | convolution fusion | flops 7257194496 | bytes 2708480 | tf_op jit(solution)/shard_map/while/body/eval_jaxpr/dot_general | solution.py:105
  225.0 10.6 %reshape_reshape.3 = f32[4,32,192,48]{3,2,1,0:T(8,128)} reshape(f32[128,8,1152]{2,1,0:T(8,128)} %copy.96) | data formatting | bytes 9437184 | tf_op jit(solution)/shard_map/reshape;reshape | solution.py:131
  235.6 8.4 %broadcast_multiply_fusion = f32[4,32,192,48]{3,2,1,0:T(8,128)S(1)} fusion(f32[4,32,192,48]{3,2,1,0:T(8,128)} %reshape_reshape.3, f32[4,32,192]{2,1,0:T(8,128)S(1)} %constant_dynamic-slice_fusion), kind=kLoop, calls=%fused_computation.21 | loop fusion | flops 1179648 | bytes 9535488 | tf_op jit(solution)/shard_map/mul | solution.py:135
  244.0 30.0 %fusion.12 = f32[4,192,32,48]{3,2,1,0:T(8,128)S(1)} fusion(f32[4,32,192,48]{3,2,1,0:T(8,128)S(1)} %broadcast_multiply_fusion, f32[4,192]{1,0:T(4,128)S(1)} %get-tuple-element.44, f32[32,32]{0,1:T(8,128)S(1)} %maximum_negate_fusion.1, f32[4,192]{1,0:T(4,128)S(1)} %get-tuple-element.43, pred[32,32]{0,1:T(8,128)(4,1)S(1)} %convert_compare_fusion.1), kind=kOutput, calls=%fused_computation.18 | convolution fusion | flops 455344128 | bytes 9448448 | tf_op jit(solution)/shard_map/fkao,faik->fiao/dot_general | solution.py:69
  274.0 18.2 %fusion.31 = f32[4,32,192,48]{3,1,2,0:T(8,128)} fusion(f32[4,192,32,48]{3,2,1,0:T(8,128)S(1)} %fusion.12, f32[4,192]{1,0:T(4,128)S(1)} %get-tuple-element.44, f32[32,32]{0,1:T(8,128)S(1)} %maximum_negate_fusion.1, f32[4,192]{1,0:T(4,128)S(1)} %get-tuple-element.43, pred[32,32]{0,1:T(8,128)(4,1)S(1)} %convert_compare_fusion.1), kind=kOutput, calls=%fused_computation.41 | convolution fusion | flops 455344128 | bytes 9448448 | tf_op jit(solution)/shard_map/fkao,faki->fiao/dot_general | solution.py:70
  292.2 11.2 %copy.99 = f32[4,32,192,48]{2,3,0,1:T(8,128)} copy(f32[4,32,192,48]{3,1,2,0:T(8,128)} %fusion.31) | data formatting | bytes 9437184 | tf_op jit(solution)/shard_map/fkao,faki->fiao/transpose | solution.py:70
  309.1 70.8 %all-to-all-done.2 = f32[4,32,192,48]{2,3,0,1:T(8,128)} async-done(((f32[4,32,192,48]{2,3,0,1:T(8,128)}), f32[4,32,192,48]{2,3,0,1:T(8,128)}, u32[]{:S(2)}, u32[]{:S(2)}) %all-to-all-start.2) | async-done | bytes 4718624 | tf_op jit(solution)/shard_map/all_to_all | solution.py:136
  380.0 10.7 %copy.136 = f32[4,4,8,192,48]{3,1,4,2,0:T(4,128)} copy(f32[4,4,8,192,48]{3,4,0,2,1:T(8,128)} %bitcast.11) | data formatting | bytes 9437184 | tf_op jit(solution)/shard_map/all_to_all | solution.py:136
  390.7 8.8 %reshape.170 = f32[4,8,6,128,48]{3,2,4,1,0:T(8,128)} reshape(f32[4,8,4,192,48]{3,2,4,1,0:T(4,128)} %bitcast.93) | data formatting | bytes 9437184 | tf_op jit(solution)/shard_map/reshape | solution.py:54
  436.6 12.4 %copy.124 = f32[4,8,6,128,48]{4,1,0,3,2:T(8,128)} copy(f32[4,8,6,128,48]{3,4,2,1,0:T(8,128)} %multiply_add_fusion) | data formatting | bytes 9437184 | tf_op jit(solution)/shard_map/reshape | solution.py:60
  449.0 15.5 %reshape.190 = f32[32,1,36864]{2,1,0:T(1,128)} reshape(f32[768,4,8,48]{3,2,1,0:T(8,128)} %bitcast.88) | data formatting | bytes 9437184
  470.2 55.7 %all-to-all-done.3 = f32[32,1,36864]{2,1,0:T(1,128)} async-done(((f32[32,1,36864]{2,1,0:T(1,128)}), f32[32,1,36864]{2,1,0:T(1,128)}, u32[]{:S(2)}, u32[]{:S(2)}) %all-to-all-start.3) | async-done | bytes 4718624 | tf_op jit(solution)/shard_map/all_to_all | solution.py:138
  525.9 15.7 %reduce.5 = f32[32,36864]{1,0:T(8,128)} reduce(f32[32,1,36864]{2,1,0:T(1,128)} %all-to-all-done.3, f32[]{:T(128)} %broadcast.205), dimensions={1}, to_apply=%all_to_all.40.reduce_sub_computation | reduce | bytes 9437188 | tf_op jit(solution)/shard_map/all_to_all | solution.py:138
  541.7 9.4 %reshape.191 = f32[768,4,8,48]{3,2,1,0:T(8,128)} reshape(f32[32,36864]{1,0:T(8,128)} %reduce.5) | data formatting | bytes 9437184
  551.1 16.4 %copy.110 = f32[4,8,24,32,48]{4,3,2,1,0:T(8,128)} copy(f32[4,8,24,32,48]{4,1,0,2,3:T(8,128)} %bitcast.87) | data formatting | bytes 9437184 | tf_op jit(solution)/shard_map/all_to_all | solution.py:138
  567.5 12.0 %reshape.172 = f32[4,8,24,12,128]{4,3,2,1,0:T(8,128)} reshape(f32[4,8,24,32,48]{4,3,2,1,0:T(8,128)} %copy.110) | data formatting | bytes 9437184 | tf_op jit(solution)/shard_map/reshape | solution.py:49
  579.5 8.4 %fusion.26 = f32[4,8,24,12,128]{4,2,3,1,0:T(8,128)S(1)} fusion(f32[4,8,24,12,128]{4,3,2,1,0:T(8,128)} %reshape.172, f32[4,8]{1,0:T(4,128)S(1)} %copy-done.7, f32[4,8]{1,0:T(4,128)S(1)} %get-tuple-element.46, f32[128,128]{1,0:T(8,128)S(1)} %maximum_negate_fusion, pred[128,128]{1,0:T(8,128)(4,1)S(1)} %convert_compare_fusion), kind=kOutput, calls=%fused_computation.33 | convolution fusion | flops 1813512192 | bytes 9519360 | tf_op jit(solution)/shard_map/flpbk,flik->flpbi/dot_general | solution.py:50
  599.0 8.2 %fusion.28 = f32[4,8,24,12,128]{4,2,3,1,0:T(8,128)} fusion(f32[4,8,24,12,128]{4,2,3,1,0:T(8,128)} %copy-done.4, f32[4,8,128]{2,1,0:T(8,128)S(1)} %get-tuple-element.47, f32[4,8,24,12]{2,3,1,0:T(8,128)S(1)} %fusion.75, f32[4,8]{1,0:T(4,128)S(1)} %copy-done.7, f32[4,8]{1,0:T(4,128)S(1)} %get-tuple-element.46, f32[128,128]{1,0:T(8,128)S(1)} %maximum_negate_fusion, ...), kind=kOutput, calls=%fused_computation.36 | convolution fusion | flops 1815871488 | bytes 9572608 | tf_op jit(solution)/shard_map/flpbk,flik->flpbi/dot_general | solution.py:50
  (84 shorter events, 112.8 us)
Async XLA Ops:
  0.0 18.6 %copy-start = (f32[2048,128]{1,0:T(8,128)S(1)}, f32[2048,128]{1,0:T(8,128)}, u32[]{:S(2)}) copy-start(f32[2048,128]{1,0:T(8,128)} %param.11) | copy-start | bytes 3145732
  0.0 2.8 copy-start.6
  0.0 2.8 copy-start.8
  6.9 44.7 %all-to-all-start = ((s32[128,32,1]{1,2,0:T(1,128)}), s32[128,32,1]{1,2,0:T(1,128)S(1)}, u32[]{:S(2)}, u32[]{:S(2)}) async-start(s32[128,32,1]{1,2,0:T(1,128)} %bitcast.4), calls=%async_computation | async-start | bytes 131072 | tf_op jit(solution)/shard_map/all_to_all | solution.py:127
  51.6 40.3 %all-to-all-start.1 = ((f32[128,1,4096]{2,1,0:T(1,128)}), f32[128,1,4096]{2,1,0:T(1,128)S(1)}, u32[]{:S(2)}, u32[]{:S(2)}) async-start(f32[128,1,4096]{2,1,0:T(1,128)} %reshape.188), calls=%async_computation.1 | async-start | bytes 4194304 | tf_op jit(solution)/shard_map/all_to_all | solution.py:126
  91.9 1.4 copy-start.3
  303.4 5.4 copy-start.5
  303.4 5.4 copy-start.7
  303.4 76.5 %all-to-all-start.2 = ((f32[4,32,192,48]{2,3,0,1:T(8,128)}), f32[4,32,192,48]{2,3,0,1:T(8,128)}, u32[]{:S(2)}, u32[]{:S(2)}) async-start(f32[4,32,192,48]{2,3,0,1:T(8,128)} %copy.99), calls=%async_computation.2 | async-start | bytes 12582912 | tf_op jit(solution)/shard_map/all_to_all | solution.py:136
  407.7 2.2 copy-start.2
  464.5 61.4 %all-to-all-start.3 = ((f32[32,1,36864]{2,1,0:T(1,128)}), f32[32,1,36864]{2,1,0:T(1,128)}, u32[]{:S(2)}, u32[]{:S(2)}) async-start(f32[32,1,36864]{2,1,0:T(1,128)} %reshape.190), calls=%async_computation.3 | async-start | bytes 9437184 | tf_op jit(solution)/shard_map/all_to_all | solution.py:138
  587.9 2.2 copy-start.4
  612.0 6.4 %copy-start.1 = (f32[2048,128]{1,0:T(8,128)S(1)}, f32[2048,128]{1,0:T(8,128)}, u32[]{:S(2)}) copy-start(f32[2048,128]{1,0:T(8,128)} %param.11) | copy-start | bytes 3145732
where the time goes:
time: 628 us; the launch traced here: 619 us
  matrix products  193 us (31%)
  local copies, waits for them, and re-layouts  182 us (29%)
  waiting for transfers between devices  154 us (25%)
  other arithmetic  50.9 us (8%)
  starting transfers between devices  32.4 us (5%)
    dot_general x8, matrix products, one_block(): return jnp.dot(values_t, hits, precision=precise_mode)  93.7 us
    all_to_all x1, waiting for transfers between devices, per_device(): lax.all_to_all(columns, 'lev', split_axis=1, concat_axis=2, tiled=True)  70.8 us
    all_to_all x1, waiting for transfers between devices, per_device(): lax.all_to_all(field, 'lat', split_axis=2, concat_axis=3, tiled=True)  55.7 us
    unnamed x22, local copies, waits for them, and re-layouts  45.3 us
    dot_general x1, matrix products, level_filter(): once = jnp.einsum('fkao,faik->fiao', field, lower, precision=precise_mode)  30 us
    all_to_all x1, waiting for transfers between devices, per_device(): lax.all_to_all(outgoing, ('lat', 'lev'), split_axis=0, concat_axis=0, til...  27.2 us
    dot_general x1, matrix products, place_rows(): return jnp.dot(placement, values, precision=precise_mode)  18.4 us
    dot_general x1, matrix products, level_filter(): return jnp.einsum('fkao,faki->fiao', once, lower, precision=precise_mode)  18.2 us
  transfers between devices with their start and end apart: 4, of which 3 were waited for; matrix products, arithmetic and copies ran while one was open for 6% of the time, Pallas kernels for 0%

commit v1 on v0

v1 whole, which is shorter than its diff:
```python
import functools

import jax
import jax.numpy as jnp
from jax import lax
from jax.experimental import pallas as pl
from jax.experimental.pallas import tpu as pltpu
from jax.sharding import PartitionSpec as P

F = 4
NLEV = 32
NLAT = 768
NLON = 1536
BANDS = 32
LEVS = 4
BAND = NLAT // BANDS
LEVQ = NLEV // LEVS
PROF = F * LEVQ
GROUP = 128 // PROF
ROWS = 32
CAP = (ROWS - 1) * GROUP
COUNT_LANE = 124
MOST_LANE = 125
STEP = 64
SEGV = 3
TILES = BAND // GROUP
PLANE = NLON
PAD = 8
GRID_ROWS = BAND * PLANE + PAD
VMEM_LIMIT = 60 * 1024 * 1024


def third(x):
    return (x * 21846) >> 16


def blocks_of(shape):
    return lax.broadcasted_iota(jnp.int32, shape, len(shape) - 1) // PROF


def send_kernel(turn, vals, owner, column, sigma, len_lev, out, xs, ax, table, decay, places, place_s, sem):
    rows = vals.shape[0]
    turn_no = turn[0]
    zeros = jnp.zeros((64, 128), jnp.float32)

    def clear(i, _):
        at = pl.ds(pl.multiple_of(i * 64, 64), 64)
        xs[at, :] = zeros
        ax[at, :] = zeros
        return 0

    d = owner[...]
    c = column[...]
    c48 = third(c >> 4)
    lat = (d & 3) * 192 + c48
    lon = (d >> 2) * 48 + (c - c48 * 48)
    band = third(lat >> 3)
    seg = lon >> 6
    grid_row = ((seg >> 3) * STEP + (lon & (STEP - 1))) * 8 + (seg & 7)
    address = (lat - band * BAND) * PLANE + grid_row + PAD

    width = 256
    r0 = lax.broadcasted_iota(jnp.int32, (width, width), 0)
    r1 = lax.broadcasted_iota(jnp.int32, (width, width), 1)
    earlier = jnp.where(r0 < r1, 1.0, 0.0).astype(jnp.bfloat16)
    band_id = lax.broadcasted_iota(jnp.int32, (BANDS, width), 0)
    place_id = lax.broadcasted_iota(jnp.int32, (128, width), 0)
    base = jnp.zeros((BANDS, 1), jnp.float32)
    found = jnp.zeros((2 * BANDS, 128), jnp.float32)
    for k in range(rows // width):
        cut = slice(k * width, (k + 1) * width)
        hot = jnp.where(band[:, cut] == band_id, 1.0, 0.0)
        before = jnp.dot(hot.astype(jnp.bfloat16), earlier, preferred_element_type=jnp.float32) + base
        rank = jnp.sum(hot * before, axis=0, keepdims=True).astype(jnp.int32) - turn_no * CAP
        base = base + jnp.sum(hot, axis=1, keepdims=True)
        valid = (rank >= 0) & (rank < CAP)
        slot = jnp.where(valid, (rank & 3) * (BANDS * ROWS) + band[:, cut] * ROWS + (rank >> 2), ROWS - 1)
        for g in range(width // 128):
            row = k * (width // 128) + g
            places[row : row + 1, :] = slot[:, g * 128 : (g + 1) * 128]
            places[row + 16 : row + 17, :] = lat[:, cut][:, g * 128 : (g + 1) * 128]
        a = address[:, cut]
        high = hot * (a >> 8).astype(jnp.float32)
        low = hot * (a & 255).astype(jnp.float32)
        both = jnp.concatenate([high, low], axis=0).astype(jnp.bfloat16)
        at_place = jnp.where(rank == place_id, 1.0, 0.0).astype(jnp.bfloat16)
        found = found + lax.dot_general(
            both, at_place, (((1,), (1,)), ((), ())), preferred_element_type=jnp.float32
        )
    copy = pltpu.make_async_copy(places, place_s, sem)
    copy.start()
    lax.fori_loop(0, xs.shape[0] // 64, clear, 0)
    headers = found[:BANDS] * 256.0 + found[BANDS:]
    lane = lax.broadcasted_iota(jnp.int32, (BANDS, 128), 1)
    left = jnp.clip(base - (turn_no * CAP).astype(jnp.float32), 0.0, float(CAP))
    most = jnp.max(base, axis=0, keepdims=True)
    headers = jnp.where(lane < CAP, headers, jnp.where(lane == COUNT_LANE, left, jnp.where(lane == MOST_LANE, most, 0.0)))

    fade = jnp.exp(-1.0 / len_lev[...])
    wide = jnp.concatenate([jnp.broadcast_to(fade[f : f + 1], (NLEV, NLAT)) for f in range(F)], axis=0)
    gain = sigma[...] * ((1.0 - wide) * (1.0 - wide))
    table[...] = jnp.transpose(gain)
    decay[...] = jnp.transpose(wide)
    copy.wait()

    def place(g, _):
        first = pl.multiple_of(g * 128, 128)
        for u in range(128):
            s = place_s[g, u]
            t = place_s[g + 16, u]
            xs[pl.ds(s, 1), :] = vals[pl.ds(first + u, 1), :] * table[pl.ds(t, 1), :]
            ax[pl.ds(s, 1), :] = decay[pl.ds(t, 1), :]
        return 0

    lax.fori_loop(0, rows // 128, place, 0)

    level = lax.broadcasted_iota(jnp.int32, (128, 128), 1) & (NLEV - 1)
    pi = lax.broadcasted_iota(jnp.int32, (256, 512), 0)
    pj = lax.broadcasted_iota(jnp.int32, (256, 512), 1)
    f_in, l_in, k_in = (pi >> 5) & 3, (pi >> 3) & 3, pi & 7
    aim = l_in * 128 + (pi >> 7) * 32 + f_in * 8 + k_in
    move = [jnp.where(pj == aim + 64 * half, 1.0, 0.0).astype(jnp.bfloat16) for half in (0, 1)]

    def smooth_levels(x, a):
        powers = [a]
        for _ in range(4):
            powers.append(powers[-1] * powers[-1])
        y = x
        for n, p in enumerate(powers):
            s = 1 << n
            y = y + jnp.where(level >= s, p, 0.0) * pltpu.roll(y, s, 1)
        for n, p in enumerate(powers):
            s = 1 << n
            y = y + jnp.where(level < NLEV - s, p, 0.0) * pltpu.roll(y, 128 - s, 1)
        return y

    def finish(i, _):
        total = jnp.zeros((128, 512), jnp.float32)
        for half in (0, 1):
            parts = []
            for q in (2 * half, 2 * half + 1):
                at = pl.ds(pl.multiple_of(q * (BANDS * ROWS) + i * 128, 128), 128)
                parts.append(smooth_levels(xs[at, :], ax[at, :]))
            x = jnp.concatenate(parts, axis=1)
            hi = x.astype(jnp.bfloat16)
            lo = (x - hi.astype(jnp.float32)).astype(jnp.bfloat16)
            total = total + jnp.dot(hi, move[half], preferred_element_type=jnp.float32)
            total = total + jnp.dot(lo, move[half], preferred_element_type=jnp.float32)
        for b in range(4):
            for l in range(LEVS):
                out[i * 4 + b, l] = total[b * ROWS : (b + 1) * ROWS, l * 128 : (l + 1) * 128]
        return 0

    lax.fori_loop(0, BANDS * ROWS // 128, finish, 0)
    for b in range(BANDS):
        for l in range(LEVS):
            out[b, l, ROWS - 1 : ROWS, :] = headers[b : b + 1]


def make_messages(turn, vals, owner, column, sigma, len_lev):
    slots = GROUP * BANDS * ROWS
    vmem = pl.BlockSpec(memory_space=pltpu.VMEM)
    return pl.pallas_call(
        send_kernel,
        out_shape=jax.ShapeDtypeStruct((BANDS, LEVS, ROWS, 128), jnp.float32),
        in_specs=[pl.BlockSpec(memory_space=pltpu.SMEM)] + [vmem] * 5,
        out_specs=vmem,
        scratch_shapes=[
            pltpu.VMEM((slots, 128), jnp.float32),
            pltpu.VMEM((slots, 128), jnp.float32),
            pltpu.VMEM((NLAT, 128), jnp.float32),
            pltpu.VMEM((NLAT, 128), jnp.float32),
            pltpu.VMEM((32, 128), jnp.int32),
            pltpu.SMEM((32, 128), jnp.int32),
            pltpu.SemaphoreType.DMA,
        ],
        compiler_params=pltpu.CompilerParams(vmem_limit_bytes=VMEM_LIMIT),
        name="make_messages",
    )(turn, vals, owner, column, sigma, len_lev)


def shift_down(x, by, sub):
    return jnp.where(sub >= by, pltpu.roll(x, by, 0), 0.0)


def shift_up(x, by, sub):
    return jnp.where(sub < 8 - by, pltpu.roll(x, 8 - by, 0), 0.0)


def grid_kernel(recv, lon_len, lat_len, ends, local, most, ga, gb, ramp, carry, ids_v, ids_s, sem):
    heads = recv[:, ROWS - 1, :]
    most[...] = jnp.max(heads, axis=0, keepdims=True)
    ids_v[...] = heads.astype(jnp.int32)
    copy = pltpu.make_async_copy(ids_v, ids_s, sem)
    copy.start()

    zeros = jnp.zeros((64, 128), jnp.float32)

    def clear(i, _):
        at = pl.ds(pl.multiple_of(i * 64, 64), 64)
        ga[at, :] = zeros
        gb[at, :] = zeros
        return 0

    lax.fori_loop(0, GRID_ROWS // 64, clear, 0)
    ga[GRID_ROWS - PAD :, :] = zeros[:PAD]
    gb[GRID_ROWS - PAD :, :] = zeros[:PAD]
    copy.wait()

    lane_block = blocks_of((1, 128))
    masks = [lane_block == q for q in range(GROUP)]
    sources = recv.shape[0]
    half = sources // 2

    def add_source(s, _):
        pair = ((s, ga), (s + half, gb))
        n = jnp.maximum(ids_s[s, COUNT_LANE], ids_s[s + half, COUNT_LANE])

        def add_rows(lo, hi):
            for j in range(lo, hi):
                where = [[ids_s[x, GROUP * j + q] for q in range(GROUP)] for x, _ in pair]
                held = [[g[pl.ds(where[i][q], 1), :] for q in range(GROUP)] for i, (_, g) in enumerate(pair)]
                for i, (x, g) in enumerate(pair):
                    row = recv[x, j : j + 1, :]
                    for q in range(GROUP):
                        pltpu.store(g.at[pl.ds(where[i][q], 1), :], held[i][q] + row, mask=masks[q])

        add_rows(0, 12)
        for lo in range(12, ROWS - 1, 4):

            @pl.when(n > GROUP * lo)
            def _():
                add_rows(lo, min(lo + 4, ROWS - 1))

        return 0

    lax.fori_loop(0, half, add_source, 0)

    il = 1.0 / lon_len[...]
    fade = jnp.broadcast_to(jnp.exp(-il), (8, 128))
    stepno = (lax.broadcasted_iota(jnp.int32, (STEP, 128), 0) + 1).astype(jnp.float32)
    ramp[...] = jnp.exp(-stepno * il)
    sub = lax.broadcasted_iota(jnp.int32, (8, 128), 0)
    subf = sub.astype(jnp.float32)
    blk = blocks_of((8, 128))
    even = (blk & 1) == 0
    lower = blk < 2
    seg_fade = [jnp.broadcast_to(jnp.exp(-il * float(STEP * m)), (8, 128)) for m in (1, 2, 4)]
    fade8 = jnp.exp(-il * float(STEP * 8))
    fade16 = jnp.exp(-il * float(STEP * 16))
    whole = 1.0 / (1.0 - jnp.exp(-il * float(NLON)))
    up_to = jnp.exp(-il * STEP * subf)
    down_to = jnp.exp(-il * STEP * (7.0 - subf))

    def at_row(lat, sv, t):
        return pl.ds(pl.multiple_of(lat * PLANE + sv * (STEP * 8) + t * 8 + PAD, 8), 8)

    def forward(t, state):
        new = []
        for i in range(TILES):
            for sv in range(SEGV):
                g = [ga[at_row(4 * i + j, sv, t), :] + gb[at_row(4 * i + j, sv, t), :] for j in range(4)]
                u = [
                    jnp.where(even, g[j], g[j + 1]) + pltpu.roll(jnp.where(even, g[j + 1], g[j]), 32, 1)
                    for j in (0, 2)
                ]
                x = jnp.where(lower, u[0], u[1]) + pltpu.roll(jnp.where(lower, u[1], u[0]), 64, 1)
                y = fade * state[i * SEGV + sv] + x
                ga[at_row(4 * i, sv, t), :] = y
                new.append(y)
        return tuple(new)

    blank = tuple(jnp.zeros((8, 128), jnp.float32) for _ in range(TILES * SEGV))
    state = lax.fori_loop(0, STEP, forward, blank)
    for i in range(TILES):
        run, tail = [], []
        for sv in range(SEGV):
            x = state[i * SEGV + sv]
            for m, by in enumerate((1, 2, 4)):
                x = x + seg_fade[m] * shift_down(x, by, sub)
            run.append(x)
            tail.append(x[7:8])
        for sv in range(SEGV):
            c = (tail[sv - 1] + fade8 * tail[sv - 2] + fade16 * tail[sv - 3]) * whole
            carry[i * SEGV + sv] = shift_down(run[sv], 1, sub) + up_to * c

    def backward(n, state):
        t = STEP - 1 - n
        r = jnp.broadcast_to(ramp[pl.ds(t, 1), :], (8, 128))
        new = []
        for i in range(TILES):
            for sv in range(SEGV):
                at = at_row(4 * i, sv, t)
                y = fade * state[i * SEGV + sv] + (ga[at, :] + r * carry[i * SEGV + sv])
                ga[at, :] = y
                new.append(y)
        return tuple(new)

    state = lax.fori_loop(0, STEP, backward, blank)
    for i in range(TILES):
        run, tail = [], []
        for sv in range(SEGV):
            x = state[i * SEGV + sv]
            for m, by in enumerate((1, 2, 4)):
                x = x + seg_fade[m] * shift_up(x, by, sub)
            run.append(x)
            tail.append(x[0:1])
        for sv in range(SEGV):
            c = (tail[(sv + 1) % 3] + fade8 * tail[(sv + 2) % 3] + fade16 * tail[sv]) * whole
            carry[i * SEGV + sv] = shift_up(run[sv], 1, sub) + down_to * c

    im = 1.0 / lat_len[...]
    one = jnp.exp(-im)
    a_lon = jnp.exp(-il)
    gain = (1.0 - a_lon) * (1.0 - a_lon) * ((1.0 - one) / (1.0 + one))

    def power(n):
        return jnp.broadcast_to(jnp.exp(-im * n.astype(jnp.float32)), (8, 128))

    near = [None] + [power(jnp.where(lane_block >= s, s, 4 - s)) for s in (1, 2, 3)]
    to_end = [power(3 - ((lane_block - s) & 3)) for s in range(4)]
    to_start = [power((lane_block - s) & 3) for s in range(4)]
    from_start = power(lane_block + 1)
    from_end = power(4 - lane_block)
    four = jnp.broadcast_to(jnp.exp(-im * 4.0), (8, 128))

    def across(p, _):
        for sv in range(SEGV):
            packed = []
            for h in (0, 1):
                t = p + h * (STEP // 2)
                r = jnp.broadcast_to(ramp[pl.ds(STEP - 1 - t, 1), :], (8, 128))
                res, up, down = [], [], []
                for i in range(TILES):
                    w = (ga[at_row(4 * i, sv, t), :] + r * carry[i * SEGV + sv]) * gain
                    rolled = [w] + [pltpu.roll(w, PROF * s, 1) for s in (1, 2, 3)]
                    res.append(w + near[1] * rolled[1] + near[2] * rolled[2] + near[3] * rolled[3])
                    up.append(sum(to_end[s] * rolled[s] for s in range(4)))
                    down.append(sum(to_start[s] * rolled[s] for s in range(4)))
                c = up[0]
                for i in range(1, TILES):
                    res[i] = res[i] + from_start * c
                    c = four * c + up[i]
                packed.append(c)
                c = down[TILES - 1]
                for i in range(TILES - 2, -1, -1):
                    res[i] = res[i] + from_end * c
                    c = four * c + down[i]
                packed.append(c)
                for i in range(TILES):
                    at = pl.ds(pl.multiple_of(i * PLANE + sv * (STEP * 8) + t * 8, 8), 8)
                    local[at, :] = res[i]
            at = pl.ds(pl.multiple_of(sv * (STEP * 4) + p * 8, 8), 8)
            ends[at, :] = jnp.where(lower, jnp.where(even, packed[0], packed[1]), jnp.where(even, packed[2], packed[3]))
        return 0

    lax.fori_loop(0, STEP // 2, across, 0)


def to_grid(recv, lon_len, lat_len):
    vmem = pl.BlockSpec(memory_space=pltpu.VMEM)
    return pl.pallas_call(
        grid_kernel,
        out_shape=(
            jax.ShapeDtypeStruct((NLON // 2, 128), jnp.float32),
            jax.ShapeDtypeStruct((TILES * PLANE, 128), jnp.float32),
            jax.ShapeDtypeStruct((1, 128), jnp.float32),
        ),
        in_specs=[vmem] * 3,
        out_specs=(vmem,) * 3,
        scratch_shapes=[
            pltpu.VMEM((GRID_ROWS, 128), jnp.float32),
            pltpu.VMEM((GRID_ROWS, 128), jnp.float32),
            pltpu.VMEM((STEP, 128), jnp.float32),
            pltpu.VMEM((TILES * SEGV, 8, 128), jnp.float32),
            pltpu.VMEM((128, 128), jnp.int32),
            pltpu.SMEM((128, 128), jnp.int32),
            pltpu.SemaphoreType.DMA,
        ],
        compiler_params=pltpu.CompilerParams(vmem_limit_bytes=VMEM_LIMIT),
        cost_estimate=pl.CostEstimate(flops=100_000_000, bytes_accessed=8_000_000, transcendentals=0),
        name="to_grid",
    )(recv, lon_len, lat_len)


def bands_kernel(ends, lat_len, out):
    im = 1.0 / lat_len[...]
    shape = ends.shape[1:]
    hop = jnp.broadcast_to(jnp.exp(-im * float(BAND)), shape)
    is_up = (blocks_of(shape) & 1) == 1
    acc = jnp.zeros(shape, jnp.float32)
    south = []
    for b in range(BANDS):
        south.append(acc)
        acc = hop * acc + ends[b]
    total = pltpu.roll(acc, PROF, 1)
    acc = jnp.zeros(shape, jnp.float32)
    for b in range(BANDS - 1, -1, -1):
        edge = jnp.exp(-im * float(BAND * (BANDS - 1 - b) + 1))
        out[b] = jnp.where(is_up, acc - edge * total, south[b])
        acc = hop * acc + ends[b]


def join_bands(ends, lat_len):
    vmem = pl.BlockSpec(memory_space=pltpu.VMEM)
    return pl.pallas_call(
        bands_kernel,
        out_shape=jax.ShapeDtypeStruct(ends.shape, jnp.float32),
        in_specs=[vmem] * 2,
        out_specs=vmem,
        compiler_params=pltpu.CompilerParams(vmem_limit_bytes=VMEM_LIMIT),
        name="join_bands",
    )(ends, lat_len)


def turn_kernel(local, control, out, flipped):
    m = pl.program_id(0)
    sv = m >> 2
    sub = (m & 3) * 2
    for i in range(TILES):
        base = i * PLANE + sv * (STEP * 8) + sub
        x = jnp.concatenate(
            [local[pl.ds(base, STEP, stride=8), :], local[pl.ds(base + 1, STEP, stride=8), :]], axis=0
        )
        flipped[i * 128 : (i + 1) * 128, :] = jnp.transpose(x)
    for v in range(PROF):
        for g in range(BAND // 8):
            x = flipped[pl.ds(v + 8 * PROF * g, 8, stride=PROF), :]
            out[v // LEVQ, v % LEVQ, 8 * g : 8 * g + 8, :] = control[v // LEVQ, v % LEVQ, 8 * g : 8 * g + 8, :] + x


def add_control(local, control):
    block = pl.BlockSpec((F, LEVQ, BAND, 128), lambda m: (0, 0, 0, m))
    return pl.pallas_call(
        turn_kernel,
        grid=(NLON // 128,),
        out_shape=jax.ShapeDtypeStruct(control.shape, jnp.float32),
        in_specs=[pl.BlockSpec((TILES * PLANE, 128), lambda m: (0, 0)), block],
        out_specs=block,
        scratch_shapes=[pltpu.VMEM((BAND * PROF, 128), jnp.float32)],
        compiler_params=pltpu.CompilerParams(vmem_limit_bytes=VMEM_LIMIT),
        cost_estimate=pl.CostEstimate(flops=20_000_000, bytes_accessed=15_000_000, transcendentals=0),
        name="add_control",
    )(local, control)


def last_kernel(lat_len, parts, joined, out, from_start, from_end, flipped):
    m = pl.program_id(0)

    @pl.when(m == 0)
    def _():
        lat = lax.broadcasted_iota(jnp.int32, (BAND, 128), 0).astype(jnp.float32)
        for v in range(PROF):
            scale = lat_len[v // LEVQ, v % LEVQ]
            from_start[v] = jnp.exp(-(lat + 1.0) / scale)
            from_end[v] = jnp.exp(-(float(BAND) - lat) / scale)

    sv = m >> 2
    sub = (m & 3) * 2
    pieces = []
    for s in (0, 1):
        x = joined[pl.ds(sv * (STEP * 4) + sub + s, STEP // 2, stride=8), :]
        pieces += [x, pltpu.roll(x, 64, 1)]
    flipped[...] = jnp.transpose(jnp.concatenate(pieces, axis=0))
    for v in range(PROF):
        south = flipped[v : v + 1, :]
        north = flipped[PROF + v : PROF + v + 1, :]
        out[v // LEVQ, v % LEVQ] = parts[v // LEVQ, v % LEVQ] + (from_start[v] * south + from_end[v] * north)


def add_bands(lat_len, parts, joined):
    block = pl.BlockSpec((F, LEVQ, BAND, 128), lambda m: (0, 0, 0, m))
    return pl.pallas_call(
        last_kernel,
        grid=(NLON // 128,),
        out_shape=jax.ShapeDtypeStruct(parts.shape, jnp.float32),
        in_specs=[
            pl.BlockSpec(memory_space=pltpu.SMEM),
            block,
            pl.BlockSpec((NLON // 2, 128), lambda m: (0, 0)),
        ],
        out_specs=block,
        scratch_shapes=[
            pltpu.VMEM((PROF, BAND, 128), jnp.float32),
            pltpu.VMEM((PROF, BAND, 128), jnp.float32),
            pltpu.VMEM((128, 128), jnp.float32),
        ],
        compiler_params=pltpu.CompilerParams(vmem_limit_bytes=VMEM_LIMIT),
        name="add_bands",
    )(lat_len, parts, joined)


def per_device(control, obs_values, obs_owner, obs_column, sigma, len_lon, len_lat, len_lev):
    owner = obs_owner.reshape(1, -1)
    column = obs_column.reshape(1, -1)
    sigma = sigma.reshape(F * NLEV, NLAT)
    lon_len = jnp.tile(len_lon.reshape(1, PROF), (1, GROUP))
    lat_len = jnp.tile(len_lat.reshape(1, PROF), (1, GROUP))

    def one_turn(turn):
        messages = make_messages(turn.reshape(1), obs_values, owner, column, sigma, len_lev)
        messages = messages.reshape(BANDS * LEVS, ROWS, 128)
        arrived = lax.all_to_all(messages, ("lat", "lev"), split_axis=0, concat_axis=0, tiled=True)
        ends, local, most = to_grid(arrived, lon_len, lat_len)
        return ends, local, most[0, MOST_LANE].astype(jnp.int32)

    ends, local, most = one_turn(jnp.int32(0))

    def more(state):
        return state[0] * CAP < most

    def next_turn(state):
        turn, ends, local = state
        more_ends, more_local, _ = one_turn(turn)
        return turn + 1, ends + more_ends, local + more_local

    _, ends, local = lax.while_loop(more, next_turn, (jnp.int32(1), ends, local))

    ends = ends.reshape(BANDS, -1, 128)
    ends = lax.all_to_all(ends, "lat", split_axis=0, concat_axis=0, tiled=True)
    joined = join_bands(ends, lat_len)
    joined = lax.all_to_all(joined, "lat", split_axis=0, concat_axis=0, tiled=True)
    parts = add_control(local, control)
    return add_bands(len_lat, parts, joined.reshape(NLON // 2, 128))


def solution(mesh):
    placed = (
        P(None, "lev", "lat", None),
        P(("lat", "lev"), None),
        P(("lat", "lev"), None),
        P(("lat", "lev")),
        P(),
        P(None, "lev"),
        P(None, "lev"),
        P(),
    )
    return jax.shard_map(
        per_device,
        mesh=mesh,
        in_specs=placed,
        out_specs=P(None, "lev", "lat", None),
        check_vma=False,
    )
```

time: 628 us -> 149 us (0.24); the launches traced: 619 us -> 149 us
  matrix products: 193 us -> 0 us
  local copies, waits for them, and re-layouts: 182 us -> 9.68 us
  waiting for transfers between devices: 154 us -> 24.2 us
  Pallas kernels: 0 us -> 84 us
  other arithmetic: 50.9 us -> 0 us
  starting transfers between devices: 32.4 us -> 15.4 us
  blocking collectives: 0 us -> 14.7 us
    dot_general x18 -> x0, matrix products: 182 us -> none  [the longest x8 93.7 us: one_block(): return jnp.dot(values_t, hits, precision=precise_mode)]
    all_to_all x4 -> x2, waiting for transfers between devices: 154 us -> 24.2 us  [the longest x1 24.2 us: one_turn(): lax.all_to_all(messages, ('lat', 'lev'), split_axis=0, concat_axis=0, til...]
    pallas_call x0 -> x5, Pallas kernels: none -> 84 us  [the longest x1 41.3 us: to_grid(): pl.pallas_call(grid_kernel, out_shape=(jax.ShapeDtypeStruct((NLON // 2, 1...]
    unnamed x22 -> x10, local copies, waits for them, and re-layouts: 45.3 us -> 2.08 us
    reshape x5 -> x0, local copies, waits for them, and re-layouts: 42.7 us -> none  [the longest x2 12.5 us: one_sweep(): blocked = field.reshape(shape[0], shape[1], blocks, BLK, shape[3])]
    all_to_all x7 -> x0, local copies, waits for them, and re-layouts: 35.7 us -> none  [the longest x1 16.4 us: per_device(): lax.all_to_all(field, 'lat', split_axis=2, concat_axis=3, tiled=True)]
    all_to_all x3 -> x0, other arithmetic: 23.8 us -> none  [the longest x1 15.7 us: per_device(): lax.all_to_all(field, 'lat', split_axis=2, concat_axis=3, tiled=True)]
    transpose x2 -> x0, local copies, waits for them, and re-layouts: 17.4 us -> none  [the longest x1 11.2 us: level_filter(): return jnp.einsum('fkao,faki->fiao', once, lower, precision=precise_mode)]
  transfers between devices with their start and end apart: 4 -> 2, of which waited for: 3 -> 1; matrix products, arithmetic and copies ran while one was open for 6% -> 4% of each run, Pallas kernels for 0% -> 8%
where the time goes in v1:
time: 149 us
  Pallas kernels  84 us (56%)
  waiting for transfers between devices  24.2 us (16%)
  starting transfers between devices  15.4 us (10%)
  blocking collectives  14.7 us (10%)
  local copies, waits for them, and re-layouts  9.68 us (6%)
    pallas_call x1, Pallas kernels, to_grid(): pl.pallas_call(grid_kernel, out_shape=(jax.ShapeDtypeStruct((NLON // 2, 1...  41.3 us
    all_to_all x1, waiting for transfers between devices, one_turn(): lax.all_to_all(messages, ('lat', 'lev'), split_axis=0, concat_axis=0, til...  24.2 us
    pallas_call x1, Pallas kernels, make_messages(): pl.pallas_call(send_kernel, out_shape=jax.ShapeDtypeStruct((BANDS, LEVS,...  19.1 us
    all_to_all x1, blocking collectives, per_device(): ends = lax.all_to_all(ends, 'lat', split_axis=0, concat_axis=0, tiled=True)  14.7 us
    pallas_call x1, Pallas kernels, add_control(): pl.pallas_call(turn_kernel, grid=(NLON // 128,), out_shape=jax.ShapeDtype...  11.9 us
    all_to_all x1, starting transfers between devices, one_turn(): lax.all_to_all(messages, ('lat', 'lev'), split_axis=0, concat_axis=0, til...  11.5 us
    pallas_call x1, Pallas kernels, add_bands(): pl.pallas_call(last_kernel, grid=(NLON // 128,), out_shape=jax.ShapeDtype...  9.85 us
    all_to_all x1, starting transfers between devices, per_device(): lax.all_to_all(joined, 'lat', split_axis=0, concat_axis=0, tiled=True)  3.9 us
  transfers between devices with their start and end apart: 2, of which 1 were waited for; matrix products, arithmetic and copies ran while one was open for 4% of the time, Pallas kernels for 8%

profile of v1, /device:TPU:1, one launch (start us, length us, event | category | flops | bytes accessed | tf_op | source)
XLA Modules:
  0.0 148.7 jit_solution(11938783421667541641)
XLA Ops:
  0.0 0.0 copy-start.1
  0.0 0.0 copy-start.2
  0.0 0.0 copy-start.5
  0.0 19.1 %make_messages.2 = f32[32,4,32,128]{3,2,1,0:T(8,128)} custom-call(s32[1]{0:T(128)} %constant.4.clone.1.turn, f32[2048,128]{1,0:T(8,128)} %vals.1, s32[1,2048]{1,0:T(1,128)} %bitcast.19, s32[1,2048]{1,0:T(1,128)} %bitcast.21, f32[128,768]{1,0:T(8,128)} %bitcast.14, f32[4,768]{1,0:T(4,128)} %len_lev.1), custom_call_target="tpu_custom_call" | custom-call | tf_op jit(solution)/shard_map/make_messages/pallas_call | solution.py:163
  19.1 11.5 %all-to-all-start.1 = ((f32[128,32,128]{2,1,0:T(8,128)}), f32[128,32,128]{2,1,0:T(8,128)S(1)}, u32[]{:S(2)}, u32[]{:S(2)}) async-start(f32[128,32,128]{2,1,0:T(8,128)} %bitcast.17), calls=%async_computation.1 | async-start | bytes 4194304 | tf_op jit(solution)/shard_map/all_to_all | solution.py:503
  30.6 0.8 tile.20
  31.4 1.2 tile.23
  32.6 1.2 tile.24
  33.8 1.3 tile.25.lat_len
  35.0 0.6 tile.21
  35.6 1.3 tile.22.lon_len
  37.0 24.2 %all-to-all-done.1.recv = f32[128,32,128]{2,1,0:T(8,128)S(1)} async-done(((f32[128,32,128]{2,1,0:T(8,128)}), f32[128,32,128]{2,1,0:T(8,128)S(1)}, u32[]{:S(2)}, u32[]{:S(2)}) %all-to-all-start.1) | async-done | bytes 2097184 | tf_op jit(solution)/shard_map/all_to_all | solution.py:503
  61.2 0.0 copy-start.3
  61.2 1.3 copy-done.3
  62.5 41.3 %to_grid.2 = (f32[768,128]{1,0:T(8,128)}, f32[9216,128]{1,0:T(8,128)}, f32[1,128]{1,0:T(1,128)}) custom-call(f32[128,32,128]{2,1,0:T(8,128)} %copy-done.3, f32[1,128]{1,0:T(1,128)} %tile.22.lon_len, f32[1,128]{1,0:T(1,128)} %tile.25.lat_len), custom_call_target="tpu_custom_call" | custom-call | flops 100000000 | bytes 8000000 | tf_op jit(solution)/shard_map/to_grid/pallas_call | solution.py:362
  103.8 1.2 slice.3
  105.6 0.0 copy-done.1
  105.6 0.0 copy-done.2
  105.6 0.0 copy-done.5
  105.6 14.7 %all_to_all.22.ends = f32[32,24,128]{2,1,0:T(8,128)} all-to-all(f32[32,24,128]{2,1,0:T(8,128)} %bitcast.16), channel_id=1, replica_groups=mesh['lat'=32,'lev'=4] {'lat'}, dimensions={0} | all-to-all | bytes 786432 | tf_op jit(solution)/shard_map/all_to_all | solution.py:520
  120.4 1.9 %join_bands.1 = f32[32,24,128]{2,1,0:T(8,128)} custom-call(f32[32,24,128]{2,1,0:T(8,128)} %all_to_all.22.ends, f32[1,128]{1,0:T(1,128)} %tile.25.lat_len), custom_call_target="tpu_custom_call" | custom-call | tf_op jit(solution)/shard_map/join_bands/pallas_call | solution.py:406
  122.3 3.9 %all-to-all-start.3 = ((f32[32,24,128]{2,1,0:T(8,128)}), f32[32,24,128]{2,1,0:T(8,128)S(1)}, u32[]{:S(2)}, u32[]{:S(2)}) async-start(f32[32,24,128]{2,1,0:T(8,128)} %join_bands.1), calls=%async_computation.3 | async-start | bytes 786432 | tf_op jit(solution)/shard_map/all_to_all | solution.py:522
  126.2 11.9 %add_control.1.parts = f32[4,8,24,1536]{3,2,1,0:T(8,128)} custom-call(f32[9216,128]{1,0:T(8,128)} %get-tuple-element.72.local, f32[4,8,24,1536]{3,2,1,0:T(8,128)} %control.1), custom_call_target="tpu_custom_call" | custom-call | flops 20000000 | bytes 15000000 | tf_op jit(solution)/shard_map/add_control/pallas_call | solution.py:434
  138.1 0.0 all-to-all-done.3
  138.1 0.0 copy-start.4
  138.1 0.7 copy-done.4
  138.8 9.9 %add_bands.1 = f32[4,8,24,1536]{3,2,1,0:T(8,128)} custom-call(f32[4,8]{1,0:T(4,128)} %lat_len.1, f32[4,8,24,1536]{3,2,1,0:T(8,128)} %add_control.1.parts, f32[768,128]{1,0:T(8,128)} %bitcast.18), custom_call_target="tpu_custom_call" | custom-call | tf_op jit(solution)/shard_map/add_bands/pallas_call | solution.py:473
  (1 shorter events, 0.0 us)
Async XLA Ops:
  0.0 105.6 %copy-start.1 = (f32[2048,128]{1,0:T(8,128)S(1)}, f32[2048,128]{1,0:T(8,128)}, u32[]{:S(2)}) copy-start(f32[2048,128]{1,0:T(8,128)} %vals.1) | copy-start | bytes 3145732
  0.0 105.6 %copy-start.2 = (f32[4,32,768]{2,1,0:T(8,128)S(1)}, f32[4,32,768]{2,1,0:T(8,128)}, u32[]{:S(2)}) copy-start(f32[4,32,768]{2,1,0:T(8,128)} %param.14) | copy-start | bytes 1179652
  0.0 105.6 %copy-start.5 = (f32[4,768]{1,0:T(4,128)S(1)}, f32[4,768]{1,0:T(4,128)}, u32[]{:S(2)}) copy-start(f32[4,768]{1,0:T(4,128)} %len_lev.1) | copy-start | bytes 36868
  19.1 42.1 %all-to-all-start.1 = ((f32[128,32,128]{2,1,0:T(8,128)}), f32[128,32,128]{2,1,0:T(8,128)S(1)}, u32[]{:S(2)}, u32[]{:S(2)}) async-start(f32[128,32,128]{2,1,0:T(8,128)} %bitcast.17), calls=%async_computation.1 | async-start | bytes 4194304 | tf_op jit(solution)/shard_map/all_to_all | solution.py:503
  61.2 1.3 copy-start.3
  122.3 15.8 %all-to-all-start.3 = ((f32[32,24,128]{2,1,0:T(8,128)}), f32[32,24,128]{2,1,0:T(8,128)S(1)}, u32[]{:S(2)}, u32[]{:S(2)}) async-start(f32[32,24,128]{2,1,0:T(8,128)} %join_bands.1), calls=%async_computation.3 | async-start | bytes 786432 | tf_op jit(solution)/shard_map/all_to_all | solution.py:522
  138.1 0.7 copy-start.4

commit v2 on v0

v2 whole, which is shorter than its diff:
```python
import jax
import jax.numpy as jnp
from jax import lax
from jax.experimental import pallas as pl
from jax.experimental.pallas import tpu as pltpu
from jax.sharding import PartitionSpec as P

F = 4
NLEV = 32
NLAT = 768
NLON = 1536
BANDS = 32
LEVS = 4
BAND = NLAT // BANDS
LEVQ = NLEV // LEVS
PROF = F * LEVQ
GROUP = 128 // PROF
ROWS = 32
CAP = (ROWS - 1) * GROUP
COUNT_LANE = 124
MOST_LANE = 125
STEP = 64
SEGV = 3
TILES = BAND // GROUP
PLANE = NLON
VMEM_LIMIT = 60 * 1024 * 1024
PAD = 8
REGION = BAND // 2 * PLANE
GRID_ROWS = REGION + PAD
HALF_CAP = CAP // 2
SWAP_LANE = 126
SAME_LANE = 127
BATCH = 2
SHARE = 2
WIDE = 4
PARTS = 3
PAIRS = BAND // 2


def third(x):
    return (x * 21846) >> 16


def blocks_of(shape):
    return lax.broadcasted_iota(jnp.int32, shape, len(shape) - 1) // PROF


def in_lanes(lengths):
    value = lax.broadcasted_iota(jnp.int32, (1, 128), 1) & (PROF - 1)
    x = jnp.ones((1, 128), jnp.float32)
    for v in range(PROF):
        x = jnp.where(value == v, lengths[v // LEVQ, v % LEVQ], x)
    return x


def in_rows(lengths, first):
    row = lax.broadcasted_iota(jnp.int32, (8, 128), 0)
    x = jnp.ones((8, 128), jnp.float32)
    for v in range(8):
        x = jnp.where(row == v, lengths[(first + v) // LEVQ, (first + v) % LEVQ], x)
    return x


def send_kernel(turn, vals, owner, column, sigma, len_lev, out, picks, work, lines, xs, places, sem, *place_s):
    rows = vals.shape[0]
    tiles = rows // 128
    turn_no = turn[0]

    d = owner[...]
    c = column[...]
    c48 = third(c >> 4)
    lat = (d & 3) * 192 + c48
    lon = (d >> 2) * 48 + (c - c48 * 48)
    band = third(lat >> 3)
    seg = lon >> 6
    grid_row = ((seg >> 3) * STEP + (lon & (STEP - 1))) * 8 + (seg & 7)
    odd = lat & 1
    address = ((lat - band * BAND) >> 1) * PLANE + grid_row + PAD

    width = 256
    r0 = lax.broadcasted_iota(jnp.int32, (width, width), 0)
    r1 = lax.broadcasted_iota(jnp.int32, (width, width), 1)
    earlier = jnp.where(r0 < r1, 1.0, 0.0).astype(jnp.bfloat16)
    band_id = lax.broadcasted_iota(jnp.int32, (BANDS, width), 0)
    place_id = lax.broadcasted_iota(jnp.int32, (128, width), 0)
    base = jnp.zeros((BANDS, 1), jnp.float32)
    half_base = jnp.zeros((2 * BANDS, 1), jnp.float32)
    found = jnp.zeros((2 * BANDS, 128), jnp.float32)
    for k in range(rows // width):
        cut = slice(k * width, (k + 1) * width)
        hot = jnp.where(band[:, cut] == band_id, 1.0, 0.0)
        before = jnp.dot(hot.astype(jnp.bfloat16), earlier, preferred_element_type=jnp.float32) + base
        rank = jnp.sum(hot * before, axis=0, keepdims=True).astype(jnp.int32) - turn_no * CAP
        base = base + jnp.sum(hot, axis=1, keepdims=True)
        now = (rank >= 0) & (rank < CAP)
        parity = odd[:, cut]
        hot = jnp.where(now, hot, 0.0)
        sides = jnp.concatenate([jnp.where(parity == 0, hot, 0.0), jnp.where(parity == 1, hot, 0.0)], axis=0)
        before = jnp.dot(sides.astype(jnp.bfloat16), earlier, preferred_element_type=jnp.float32) + half_base
        rank = jnp.sum(sides * before, axis=0, keepdims=True).astype(jnp.int32)
        half_base = half_base + jnp.sum(sides, axis=1, keepdims=True)
        swapped = rank >= HALF_CAP
        pos = jnp.where(swapped, CAP - 1 - rank, rank)
        q = 2 * (pos & 1) + jnp.where(swapped, 1 - parity, parity)
        row = pos >> 1
        slot = jnp.where(now, q * (BANDS * ROWS) + band[:, cut] * ROWS + row, ROWS - 1)
        for g in range(width // 128):
            n = k * (width // 128) + g
            places[n : n + 1, :] = slot[:, g * 128 : (g + 1) * 128]
            places[tiles + n : tiles + n + 1, :] = lat[:, cut][:, g * 128 : (g + 1) * 128]
        a = address[:, cut] + jnp.where(swapped, REGION, 0)
        high = hot * (a >> 8).astype(jnp.float32)
        low = hot * (a & 255).astype(jnp.float32)
        both = jnp.concatenate([high, low], axis=0).astype(jnp.bfloat16)
        at_place = jnp.where(row * GROUP + q == place_id, 1.0, 0.0).astype(jnp.bfloat16)
        found = found + lax.dot_general(
            both, at_place, (((1,), (1,)), ((), ())), preferred_element_type=jnp.float32
        )
    copies = [
        pltpu.make_async_copy(places.at[pl.ds(n, 1), :], place_s[n], sem.at[n]) for n in range(tiles)
    ]
    for copy in copies:
        copy.start()
    headers = found[:BANDS] * 256.0 + found[BANDS:]
    lane = lax.broadcasted_iota(jnp.int32, (BANDS, 128), 1)
    most_side = jnp.maximum(half_base[:BANDS], half_base[BANDS:])
    left = jnp.minimum(2.0 * most_side, float(CAP))
    swaps = jnp.where(most_side > float(HALF_CAP), 1.0, 0.0)
    most = jnp.max(base, axis=0, keepdims=True)
    headers = jnp.where(lane < CAP, headers, 0.0)
    headers = jnp.where(lane == COUNT_LANE, left, headers)
    headers = jnp.where(lane == MOST_LANE, most, headers)
    headers = jnp.where(lane == SWAP_LANE, swaps, headers)

    sig = sigma[...]
    sig_hi = sig.astype(jnp.bfloat16)
    picks[0:128, :] = sig_hi
    picks[128:256, :] = (sig - sig_hi.astype(jnp.float32)).astype(jnp.bfloat16)
    fade = jnp.exp(-1.0 / len_lev[...])
    fade = jnp.concatenate([fade, fade], axis=0)
    f_hi = fade.astype(jnp.bfloat16).astype(jnp.float32)
    f_mid = (fade - f_hi).astype(jnp.bfloat16).astype(jnp.float32)
    f_lo = fade - f_hi - f_mid
    picks[256:288, :] = jnp.concatenate([f_hi, f_mid, f_lo, jnp.zeros_like(fade)], axis=0).astype(jnp.bfloat16)
    lat_id = lax.broadcasted_iota(jnp.int32, (NLAT, width), 0)

    def smooth_levels(k, _):
        which = jnp.concatenate([places[pl.ds(tiles + 2 * k + g, 1), :] for g in (0, 1)], axis=1)
        at_lat = jnp.where(lat_id == which, 1.0, 0.0).astype(jnp.bfloat16)
        got = jnp.dot(picks[...], at_lat, preferred_element_type=jnp.float32)
        for g in (0, 1):
            lanes = slice(g * 128, (g + 1) * 128)
            at = pl.ds(pl.multiple_of(k * width + g * 128, 128), 128)
            side = work.at[g]
            side[0:128, :] = jnp.transpose(vals[at, :]) * (got[0:128, lanes] + got[128:256, lanes])
            a = got[256:260, lanes] + got[264:268, lanes] + got[272:276, lanes]
            y = [side[pl.ds(0, F, stride=NLEV), :]]
            for n in range(1, NLEV):
                y.append(a * y[-1] + side[pl.ds(n, F, stride=NLEV), :])
            gain = (1.0 - a) * (1.0 - a)
            w = y[-1]
            for n in range(NLEV - 1, -1, -1):
                if n < NLEV - 1:
                    w = a * w + y[n]
                side[pl.ds(128 + n // LEVQ * PROF + n % LEVQ, F, stride=LEVQ), :] = w * gain
            lines[at, :] = jnp.transpose(side[128:, :])
        return 0

    lax.fori_loop(0, rows // width, smooth_levels, 0)

    zeros = jnp.zeros((128, 128), jnp.float32)

    def clear(i, _):
        xs[pl.ds(pl.multiple_of(i * 128, 128), 128), :] = zeros
        return 0

    lax.fori_loop(0, xs.shape[0] // 128, clear, 0)
    for copy in copies:
        copy.wait()

    def place(n, _):
        for u in range(4):
            r = n * 4 + u
            to = [place_s[g][0, r] for g in range(tiles)]
            for g in range(tiles):
                xs[pl.ds(to[g], 1), :] = lines[pl.ds(g * 128 + r, 1), :]
        return 0

    lax.fori_loop(0, 128 // 4, place, 0)

    blk = blocks_of((ROWS, 128))
    even = (blk & 1) == 0
    lower = blk < 2

    def finish(n, _):
        done = []
        for b in (2 * n, 2 * n + 1):
            x = [xs[pl.ds(pl.multiple_of(q * (BANDS * ROWS) + b * ROWS, ROWS), ROWS), :] for q in range(GROUP)]
            first = [jnp.where(lower, x[q], pltpu.roll(x[q + 2], 64, 1)) for q in (0, 1)]
            last = [jnp.where(lower, pltpu.roll(x[q], 64, 1), x[q + 2]) for q in (0, 1)]
            for l, (u, w) in ((0, first), (2, last)):
                done.append((b, l, jnp.where(even, u, pltpu.roll(w, 32, 1))))
                done.append((b, l + 1, jnp.where(even, pltpu.roll(u, 96, 1), w)))
        for b, l, x in done:
            out[b, l] = x
        return 0

    lax.fori_loop(0, BANDS // 2, finish, 0)
    for b in range(BANDS):
        for l in range(LEVS):
            out[b, l, ROWS - 1 : ROWS, :] = headers[b : b + 1]


def make_messages(turn, vals, owner, column, sigma, len_lev):
    rows = vals.shape[0]
    vmem = pl.BlockSpec(memory_space=pltpu.VMEM)
    return pl.pallas_call(
        send_kernel,
        out_shape=jax.ShapeDtypeStruct((BANDS, LEVS, ROWS, 128), jnp.float32),
        in_specs=[pl.BlockSpec(memory_space=pltpu.SMEM)] + [vmem] * 5,
        out_specs=vmem,
        scratch_shapes=[
            pltpu.VMEM((288, NLAT), jnp.bfloat16),
            pltpu.VMEM((2, 256, 128), jnp.float32),
            pltpu.VMEM((rows, 128), jnp.float32),
            pltpu.VMEM((GROUP * BANDS * ROWS, 128), jnp.float32),
            pltpu.VMEM((rows // 64, 128), jnp.int32),
            pltpu.SemaphoreType.DMA((rows // 128,)),
        ]
        + [pltpu.SMEM((1, 128), jnp.int32)] * (rows // 128),
        compiler_params=pltpu.CompilerParams(vmem_limit_bytes=VMEM_LIMIT),
        name="make_messages",
    )(turn, vals, owner, column, sigma, len_lev)


def fold_lanes(a, b, first, by):
    return jnp.where(first, a, b) + pltpu.roll(jnp.where(first, b, a), by, 1)


def shift_down(x, by, sub):
    return jnp.where(sub >= by, pltpu.roll(x, by, 0), 0.0)


def shift_up(x, by, sub):
    return jnp.where(sub < 8 - by, pltpu.roll(x, 8 - by, 0), 0.0)


def grid_kernel(recv, lat_len, ends, pairs, most, ga, gb, ups, downs, ids_v, sem, out_sem, *ids_s):
    heads = recv[:, ROWS - 1, :]
    lane = lax.broadcasted_iota(jnp.int32, (128, 128), 1)
    heads = jnp.where(lane == MOST_LANE, jnp.max(heads, axis=0, keepdims=True), heads)
    ids = jnp.transpose(heads).astype(jnp.int32)
    same = jnp.zeros((8, 128), jnp.bool_)
    for m in range(0, 128, 16):
        a, b = ids[m : m + 8], ids[m + 8 : m + 16]
        turned = pltpu.roll(b, 4, 0)
        same = same | ((a >= PAD) & ((a == pltpu.roll(a, 4, 0)) | (a == b) | (a == turned)))
        same = same | ((b >= PAD) & (b == turned))
    same = jnp.max(jnp.where(same, 1, 0), axis=0, keepdims=True)
    ids_v[...] = ids
    ids_v[SAME_LANE : SAME_LANE + 1, :] = same
    copies = [
        pltpu.make_async_copy(ids_v.at[pl.ds(GROUP * j, GROUP), :], ids_s[j], sem.at[j]) for j in range(ROWS)
    ]
    for copy in copies:
        copy.start()
    zeros = jnp.zeros((256, 128), jnp.float32)

    def clear(i, _):
        at = pl.ds(pl.multiple_of(PAD + i * 256, 8), 256)
        ga[at, :] = zeros
        gb[at, :] = zeros
        return 0

    lax.fori_loop(0, REGION // 256, clear, 0)
    ga[:PAD, :] = zeros[:PAD]
    gb[:PAD, :] = zeros[:PAD]
    for copy in copies:
        copy.wait()
    tail = ids_s[ROWS - 1]
    most[0] = tail[MOST_LANE - CAP, 0]

    lane_block = blocks_of((1, 128))
    masks = [lane_block == q for q in range(GROUP)]
    half = recv.shape[0] // 2

    def add_source(s, _):
        pair = ((s, ga), (s + half, gb))
        n = jnp.maximum(tail[COUNT_LANE - CAP, s], tail[COUNT_LANE - CAP, s + half])
        swaps = tail[SWAP_LANE - CAP, s] + tail[SWAP_LANE - CAP, s + half]
        sames = tail[SAME_LANE - CAP, s] + tail[SAME_LANE - CAP, s + half]

        def add_rows(lo, hi, batch):
            items = [(range(j, min(j + batch, hi)), x, g) for j in range(lo, hi, batch) for x, g in pair]

            def read(item):
                js, x, g = item
                at = [[pl.ds(ids_s[j][q, x], 1) for q in range(GROUP)] for j in js]
                return at, [[g[a, :] for a in some] for some in at], [recv[x, j : j + 1, :] for j in js]

            ahead = read(items[0])
            for k, (_, _, g) in enumerate(items):
                at, held, row = ahead
                if k + 1 < len(items):
                    ahead = read(items[k + 1])
                for m in range(len(row)):
                    for q in range(GROUP):
                        pltpu.store(g.at[at[m][q], :], held[m][q] + row[m], mask=masks[q])

        def add_message(batch):
            add_rows(0, 12, batch)
            for lo in range(12, ROWS - 1, 4):

                @pl.when(n > GROUP * lo)
                def _():
                    add_rows(lo, min(lo + 4, ROWS - 1), batch)

        @pl.when(swaps + sames == 0)
        def _():
            add_message(BATCH)

        @pl.when((swaps == 0) & (sames > 0))
        def _():
            add_message(1)

        @pl.when(swaps > 0)
        def _():
            for x, g in pair:
                for j in range(ROWS - 1):
                    row = recv[x, j : j + 1, :]
                    turned = pltpu.roll(row, PROF, 1)
                    for q in range(GROUP):
                        to = ids_s[j][q, x]
                        far = to >= GRID_ROWS
                        for at, what, mask in (
                            (jnp.where(far, 0, to), row, masks[q]),
                            (jnp.where(far, to - REGION, 0), turned, masks[(q + 1) % GROUP]),
                        ):
                            at = pl.ds(at, 1)
                            pltpu.store(g.at[at, :], g[at, :] + what, mask=mask)

        return 0

    lax.fori_loop(0, half, add_source, 0)

    im = 1.0 / in_lanes(lat_len)

    def power(n):
        return jnp.broadcast_to(jnp.exp(-im * n.astype(jnp.float32)), (8, 128))

    parity = lane_block & 1
    to_end = [power(BAND - 1 - 2 * n - parity) for n in range(PAIRS)]
    to_start = [power(2 * n + parity) for n in range(PAIRS)]
    out_copies = []
    for part in range(PARTS):

        def gather(r, _):
            row = part * (PLANE // PARTS) + r * 8
            at = [pl.ds(pl.multiple_of(PAD + n * PLANE + row, 8), 8) for n in range(PAIRS)]
            cells = [ga[a, :] + gb[a, :] for a in at]
            up = down = None
            for n, x in enumerate(cells):
                up = to_end[n] * x if n == 0 else up + to_end[n] * x
                down = to_start[n] * x if n == 0 else down + to_start[n] * x
            for a, x in zip(at, cells):
                ga[a, :] = x
            here = pl.ds(pl.multiple_of(row, 8), 8)
            ups[here, :] = up
            downs[here, :] = down
            return 0

        lax.fori_loop(0, PLANE // PARTS // 8, gather, 0)
        for n in range(PAIRS):
            first = n * PLANE + part * (PLANE // PARTS)
            out_copies.append(
                pltpu.make_async_copy(
                    ga.at[pl.ds(PAD + first, PLANE // PARTS), :],
                    pairs.at[pl.ds(first, PLANE // PARTS), :],
                    out_sem.at[part * PAIRS + n],
                )
            )
            out_copies[-1].start()

    blk = blocks_of((8, 128))
    even = (blk & 1) == 0
    lower = blk < 2

    def pack(k, _):
        done = []
        for u in range(16):
            p = k * 16 + u
            row = (p >> 5) * (STEP * 8) + (p & 31) * 8
            sums = []
            for h in (0, 1):
                at = pl.ds(pl.multiple_of(row + h * (STEP * 4), 8), 8)
                sums.append(fold_lanes(ups[at, :], downs[at, :], even, 32))
            done.append(fold_lanes(sums[0], sums[1], lower, 64))
        for u, x in enumerate(done):
            ends[pl.ds(pl.multiple_of((k * 16 + u) * 8, 8), 8), :] = x
        return 0

    lax.fori_loop(0, SEGV * (STEP // 2) // 16, pack, 0)
    for copy in out_copies:
        copy.wait()


def to_grid(recv, lat_len):
    vmem = pl.BlockSpec(memory_space=pltpu.VMEM)
    smem = pl.BlockSpec(memory_space=pltpu.SMEM)
    return pl.pallas_call(
        grid_kernel,
        out_shape=(
            jax.ShapeDtypeStruct((NLON // 2, 128), jnp.float32),
            jax.ShapeDtypeStruct((REGION, 128), jnp.float32),
            jax.ShapeDtypeStruct((1,), jnp.int32),
        ),
        in_specs=[vmem, smem],
        out_specs=(vmem, pl.BlockSpec(memory_space=pl.ANY), smem),
        scratch_shapes=[
            pltpu.VMEM((GRID_ROWS, 128), jnp.float32),
            pltpu.VMEM((GRID_ROWS, 128), jnp.float32),
            pltpu.VMEM((PLANE, 128), jnp.float32),
            pltpu.VMEM((PLANE, 128), jnp.float32),
            pltpu.VMEM((128, 128), jnp.int32),
            pltpu.SemaphoreType.DMA((ROWS,)),
            pltpu.SemaphoreType.DMA((PARTS * PAIRS,)),
        ]
        + [pltpu.SMEM((GROUP, 128), jnp.int32)] * ROWS,
        compiler_params=pltpu.CompilerParams(vmem_limit_bytes=VMEM_LIMIT),
        name="to_grid",
    )(recv, lat_len)


def circle_carry(last, fades, backward):
    il, seg_fade, fade8, fade16, whole, sub = fades
    run, tail = [], []
    for x in last:
        for m, by in enumerate((1, 2, 4)):
            x = x + seg_fade[m] * (shift_up if backward else shift_down)(x, by, sub)
        run.append(x)
        tail.append(x[0:1] if backward else x[7:8])
    entering = []
    for sv in range(SEGV):
        order = [tail[(sv + n) % 3] if backward else tail[(sv - n) % 3] for n in (1, 2, 3)]
        c = (order[0] + fade8 * order[1] + fade16 * order[2]) * whole
        if backward:
            entering.append(shift_up(run[sv], 1, sub) + jnp.exp(-il * (STEP * (7.0 - sub.astype(jnp.float32)))) * c)
        else:
            entering.append(shift_down(run[sv], 1, sub) + jnp.exp(-il * (STEP * sub.astype(jnp.float32))) * c)
    return entering


def circle_fades(il):
    sub = lax.broadcasted_iota(jnp.int32, (8, 128), 0)
    seg_fade = [jnp.broadcast_to(jnp.exp(-il * float(STEP * m)), (8, 128)) for m in (1, 2, 4)]
    fade8 = jnp.exp(-il * float(STEP * 8))
    fade16 = jnp.exp(-il * float(STEP * 16))
    whole = 1.0 / (1.0 - jnp.exp(-il * float(NLON)))
    return il, seg_fade, fade8, fade16, whole, sub


def total_gain(il, im):
    one_lon, one_lat = jnp.exp(-il), jnp.exp(-im)
    return (1.0 - one_lon) * (1.0 - one_lon) * ((1.0 - one_lat) / (1.0 + one_lat))


def smooth_kernel(pairs, lon_len, local, done, ramp, carry):
    il = 1.0 / in_lanes(lon_len)
    fade = jnp.broadcast_to(jnp.exp(-il), (8, 128))
    stepno = (lax.broadcasted_iota(jnp.int32, (STEP, 128), 0) + 1).astype(jnp.float32)
    ramp[...] = jnp.exp(-stepno * il)
    fades = circle_fades(il)
    lower = blocks_of((8, 128)) < 2
    vectors = [(i, sv) for i in range(SHARE) for sv in range(SEGV)]

    def at_row(i, sv, t):
        return pl.ds(pl.multiple_of(i * PLANE + sv * (STEP * 8) + t * 8, 8), 8)

    def forward(n, state):
        cells = []
        for u in range(4):
            cells.append(
                [
                    fold_lanes(
                        pairs[at_row(2 * i, sv, n * 4 + u), :], pairs[at_row(2 * i + 1, sv, n * 4 + u), :], lower, 64
                    )
                    for i, sv in vectors
                ]
            )
        for u in range(4):
            state = tuple(fade * y + x for y, x in zip(state, cells[u]))
            cells[u] = state
        for u in range(4):
            for (i, sv), y in zip(vectors, cells[u]):
                local[at_row(i, sv, n * 4 + u), :] = y
        return state

    blank = tuple(jnp.zeros((8, 128), jnp.float32) for _ in vectors)
    state = lax.fori_loop(0, STEP // 4, forward, blank)
    for i in range(SHARE):
        for sv, x in enumerate(circle_carry(state[i * SEGV : (i + 1) * SEGV], fades, False)):
            carry[i * SEGV + sv] = x

    def backward(n, state):
        cells = []
        for u in range(4):
            t = STEP - 1 - n * 4 - u
            r = jnp.broadcast_to(ramp[pl.ds(t, 1), :], (8, 128))
            cells.append([local[at_row(i, sv, t), :] + r * carry[k] for k, (i, sv) in enumerate(vectors)])
        for u in range(4):
            state = tuple(fade * y + x for y, x in zip(state, cells[u]))
            cells[u] = state
        for u in range(4):
            for (i, sv), y in zip(vectors, cells[u]):
                local[at_row(i, sv, STEP - 1 - n * 4 - u), :] = y
        return state

    state = lax.fori_loop(0, STEP // 4, backward, blank)
    for i in range(SHARE):
        for sv, x in enumerate(circle_carry(state[i * SEGV : (i + 1) * SEGV], fades, True)):
            carry[i * SEGV + sv] = x

    def finish(n, _):
        cells = []
        for u in range(4):
            r = jnp.broadcast_to(ramp[pl.ds(STEP - 1 - n * 4 - u, 1), :], (8, 128))
            cells.append([local[at_row(i, sv, n * 4 + u), :] + r * carry[k] for k, (i, sv) in enumerate(vectors)])
        for u in range(4):
            for (i, sv), y in zip(vectors, cells[u]):
                local[at_row(i, sv, n * 4 + u), :] = y
        return 0

    lax.fori_loop(0, STEP // 4, finish, 0)
    done[...] = fade


def smooth_band(pairs, lon_len):
    return pl.pallas_call(
        smooth_kernel,
        grid=(TILES // SHARE,),
        out_shape=(
            jax.ShapeDtypeStruct((TILES * PLANE, 128), jnp.float32),
            jax.ShapeDtypeStruct((8, 128), jnp.float32),
        ),
        in_specs=[
            pl.BlockSpec((2 * SHARE * PLANE, 128), lambda n: (n, 0)),
            pl.BlockSpec(memory_space=pltpu.SMEM),
        ],
        out_specs=(
            pl.BlockSpec((SHARE * PLANE, 128), lambda n: (n, 0)),
            pl.BlockSpec(memory_space=pltpu.VMEM),
        ),
        scratch_shapes=[
            pltpu.VMEM((STEP, 128), jnp.float32),
            pltpu.VMEM((SHARE * SEGV, 8, 128), jnp.float32),
        ],
        compiler_params=pltpu.CompilerParams(vmem_limit_bytes=VMEM_LIMIT),
        cost_estimate=pl.CostEstimate(flops=20_000_000, bytes_accessed=14_000_000, transcendentals=0),
        name="smooth_band",
    )(pairs, lon_len)


def bands_kernel(ends, lat_len, _, out):
    im = 1.0 / in_lanes(lat_len)
    shape = ends.shape[1:]
    hop = jnp.broadcast_to(jnp.exp(-im * float(BAND)), shape)
    is_up = (blocks_of(shape) & 1) == 1
    acc = jnp.zeros(shape, jnp.float32)
    south = []
    for b in range(BANDS):
        south.append(acc)
        acc = hop * acc + ends[b]
    total = pltpu.roll(acc, PROF, 1)
    acc = jnp.zeros(shape, jnp.float32)
    for b in range(BANDS - 1, -1, -1):
        edge = jnp.exp(-im * float(BAND * (BANDS - 1 - b) + 1))
        out[b] = jnp.where(is_up, acc - edge * total, south[b])
        acc = hop * acc + ends[b]


def join_bands(ends, lat_len, after):
    vmem = pl.BlockSpec(memory_space=pltpu.VMEM)
    return pl.pallas_call(
        bands_kernel,
        out_shape=jax.ShapeDtypeStruct(ends.shape, jnp.float32),
        in_specs=[vmem, pl.BlockSpec(memory_space=pltpu.SMEM), pl.BlockSpec(memory_space=pl.ANY)],
        out_specs=vmem,
        compiler_params=pltpu.CompilerParams(vmem_limit_bytes=VMEM_LIMIT),
        name="join_bands",
    )(ends, lat_len, after)


def turn_kernel(local, control, lon_len, lat_len, out, flipped):
    m = pl.program_id(0)
    for side in range(WIDE):
        sub = (m % (4 // WIDE) * WIDE + side) * 2
        for i in range(TILES):
            x = jnp.concatenate(
                [local[i, pl.ds(sub, STEP, stride=8), :], local[i, pl.ds(sub + 1, STEP, stride=8), :]], axis=0
            )
            flipped[side, i * 128 : (i + 1) * 128, :] = jnp.transpose(x)
    for o in range(0, PROF, 8):
        il = 1.0 / in_rows(lon_len, o)
        im = 1.0 / in_rows(lat_len, o)
        fade = jnp.exp(-im)
        gain = total_gain(il, im)
        for side in range(WIDE):
            x = [flipped[side, n * PROF + o : n * PROF + o + 8, :] for n in range(BAND)]
            south = [x[0]]
            for n in range(1, BAND):
                south.append(fade * south[-1] + x[n])
            north = jnp.zeros((8, 128), jnp.float32)
            for n in range(BAND - 1, -1, -1):
                north = fade * north
                flipped[side, n * PROF + o : n * PROF + o + 8, :] = (south[n] + north) * gain
                north = north + x[n]
    for v in range(PROF):
        for g in range(BAND // 8):
            for side in range(WIDE):
                x = flipped[side, pl.ds(v + 8 * PROF * g, 8, stride=PROF), :]
                f, k, lats, lanes = v // LEVQ, v % LEVQ, slice(8 * g, 8 * g + 8), slice(128 * side, 128 * side + 128)
                out[f, k, lats, lanes] = control[f, k, lats, lanes] + x


def add_control(local, control, lon_len, lat_len):
    block = pl.BlockSpec((F, LEVQ, BAND, 128 * WIDE), lambda m: (0, 0, 0, m))
    smem = pl.BlockSpec(memory_space=pltpu.SMEM)
    return pl.pallas_call(
        turn_kernel,
        grid=(NLON // 128 // WIDE,),
        out_shape=jax.ShapeDtypeStruct(control.shape, jnp.float32),
        in_specs=[
            pl.BlockSpec((TILES, STEP * 8, 128), lambda m: (0, m // (4 // WIDE), 0)),
            block,
            smem,
            smem,
        ],
        out_specs=block,
        scratch_shapes=[pltpu.VMEM((WIDE, BAND * PROF, 128), jnp.float32)],
        compiler_params=pltpu.CompilerParams(vmem_limit_bytes=VMEM_LIMIT),
        cost_estimate=pl.CostEstimate(flops=20_000_000, bytes_accessed=15_000_000, transcendentals=0),
        name="add_control",
    )(local.reshape(TILES, PLANE, 128), control, lon_len, lat_len)


def last_kernel(lat_len, lon_len, parts, joined, out, held, from_start, from_end, ys, south, north, sem):
    half = STEP // 2
    per = LEVQ // 4
    chunks = [(k // 4, pl.ds(k % 4 * per, per)) for k in range(F * 4)]
    fetches = [pltpu.make_async_copy(parts.at[c], held.at[c], sem.at[0, k]) for k, c in enumerate(chunks)]
    stores = [pltpu.make_async_copy(held.at[c], out.at[c], sem.at[1, k]) for k, c in enumerate(chunks)]
    for copy in fetches:
        copy.start()

    lat = lax.broadcasted_iota(jnp.int32, (BAND, 128), 0).astype(jnp.float32)
    for v in range(PROF):
        scale = lat_len[v // LEVQ, v % LEVQ]
        from_start[v] = jnp.exp(-(lat + 1.0) / scale)
        from_end[v] = jnp.exp(-(float(BAND) - lat) / scale)

    il = 1.0 / in_lanes(lon_len)
    im = 1.0 / in_lanes(lat_len)
    fade = jnp.broadcast_to(jnp.exp(-il), (8, 128))
    fades = circle_fades(il)
    half_fade = jnp.broadcast_to(jnp.exp(-il * float(half)), (8, 128))
    first = blocks_of((8, 128)) < 2
    gain = total_gain(il, im)

    def rows_at(sv, p):
        return slice(sv * (half * 8) + p * 8, sv * (half * 8) + p * 8 + 8)

    def enter(last, backward):
        other = [pltpu.roll(x, 64, 1) for x in last]
        early = jnp.logical_not(first) if backward else first
        full = [jnp.where(early, o + half_fade * x, x + half_fade * o) for x, o in zip(last, other)]
        into = circle_carry(full, fades, backward)
        return [jnp.where(early, c, o + half_fade * c) for c, o in zip(into, other)]

    y = [jnp.zeros((8, 128), jnp.float32)] * SEGV
    for p in range(half):
        for sv in range(SEGV):
            y[sv] = fade * y[sv] + joined[rows_at(sv, p), :]
            ys[rows_at(sv, p), :] = y[sv]
    into = enter(y, False)
    y = [jnp.zeros((8, 128), jnp.float32)] * SEGV
    for p in range(half - 1, -1, -1):
        r = jnp.exp(-il * float(p + 1))
        for sv in range(SEGV):
            y[sv] = fade * y[sv] + (ys[rows_at(sv, p), :] + r * into[sv])
            ys[rows_at(sv, p), :] = y[sv]
    into = enter(y, True)
    for p in range(half):
        r = jnp.exp(-il * float(half - p))
        for sv in range(SEGV):
            ys[rows_at(sv, p), :] = (ys[rows_at(sv, p), :] + r * into[sv]) * gain
    for m in range(NLON // 128):
        pieces = []
        for s in (0, 1):
            x = ys[pl.ds(m // 4 * (half * 8) + m % 4 * 2 + s, half, stride=8), :]
            pieces += [x, pltpu.roll(x, 64, 1)]
        x = jnp.transpose(jnp.concatenate(pieces, axis=0))
        south[m] = x[0:PROF]
        north[m] = x[PROF : 2 * PROF]

    for n, fetch in enumerate(fetches):
        fetch.wait()
        for k in range(per):
            v = n * per + k
            f, level = v // LEVQ, v % LEVQ
            up, down = from_start[v], from_end[v]
            for m in range(NLON // 128):
                lanes = slice(m * 128, (m + 1) * 128)
                held[f, level, :, lanes] = held[f, level, :, lanes] + (
                    up * south[m, v : v + 1, :] + down * north[m, v : v + 1, :]
                )
        stores[n].start()
    for copy in stores:
        copy.wait()


def add_bands(lat_len, lon_len, parts, joined):
    smem = pl.BlockSpec(memory_space=pltpu.SMEM)
    vmem = pl.BlockSpec(memory_space=pltpu.VMEM)
    hbm = pl.BlockSpec(memory_space=pl.ANY)
    return pl.pallas_call(
        last_kernel,
        out_shape=jax.ShapeDtypeStruct(parts.shape, jnp.float32),
        in_specs=[smem, smem, hbm, vmem],
        out_specs=hbm,
        scratch_shapes=[
            pltpu.VMEM(parts.shape, jnp.float32),
            pltpu.VMEM((PROF, BAND, 128), jnp.float32),
            pltpu.VMEM((PROF, BAND, 128), jnp.float32),
            pltpu.VMEM((NLON // 2, 128), jnp.float32),
            pltpu.VMEM((NLON // 128, PROF, 128), jnp.float32),
            pltpu.VMEM((NLON // 128, PROF, 128), jnp.float32),
            pltpu.SemaphoreType.DMA((2, F * 4)),
        ],
        compiler_params=pltpu.CompilerParams(vmem_limit_bytes=VMEM_LIMIT),
        name="add_bands",
    )(lat_len, lon_len, parts, joined)


def per_device(control, obs_values, obs_owner, obs_column, sigma, len_lon, len_lat, len_lev):
    owner = obs_owner.reshape(1, -1)
    column = obs_column.reshape(1, -1)
    sigma = sigma.reshape(F * NLEV, NLAT)
    def one_turn(turn):
        messages = make_messages(turn.reshape(1), obs_values, owner, column, sigma, len_lev)
        messages = messages.reshape(BANDS * LEVS, ROWS, 128)
        arrived = lax.all_to_all(messages, ("lat", "lev"), split_axis=0, concat_axis=0, tiled=True)
        ends, grid, most = to_grid(arrived, len_lat)
        return ends, grid, most[0]

    ends, grid, most = one_turn(jnp.int32(0))

    def more(state):
        return state[0] * CAP < most

    def next_turn(state):
        turn, ends, grid = state
        more_ends, more_grid, _ = one_turn(turn)
        return turn + 1, ends + more_ends, grid + more_grid

    _, ends, grid = lax.while_loop(more, next_turn, (jnp.int32(1), ends, grid))

    ends = ends.reshape(BANDS, -1, 128)
    ends = lax.all_to_all(ends, "lat", split_axis=0, concat_axis=0, tiled=True)
    local, done = smooth_band(grid, len_lon)
    joined = join_bands(ends, len_lat, done)
    joined = lax.all_to_all(joined, "lat", split_axis=0, concat_axis=0, tiled=True)
    parts = add_control(local, control, len_lon, len_lat)
    return add_bands(len_lat, len_lon, parts, joined.reshape(NLON // 2, 128))


def solution(mesh):
    placed = (
        P(None, "lev", "lat", None),
        P(("lat", "lev"), None),
        P(("lat", "lev"), None),
        P(("lat", "lev")),
        P(),
        P(None, "lev"),
        P(None, "lev"),
        P(),
    )
    return jax.shard_map(
        per_device,
        mesh=mesh,
        in_specs=placed,
        out_specs=P(None, "lev", "lat", None),
        check_vma=False,
    )
```

time: 628 us -> 122 us (0.19); the launches traced: 619 us -> 122 us
  matrix products: 193 us -> 0 us
  local copies, waits for them, and re-layouts: 182 us -> 2.82 us
  waiting for transfers between devices: 154 us -> 31.7 us
  Pallas kernels: 0 us -> 63.5 us
  other arithmetic: 50.9 us -> 0 us
  starting transfers between devices: 32.4 us -> 22.6 us
    dot_general x18 -> x0, matrix products: 182 us -> none  [the longest x8 93.7 us: one_block(): return jnp.dot(values_t, hits, precision=precise_mode)]
    all_to_all x4 -> x3, waiting for transfers between devices: 154 us -> 31.7 us  [the longest x1 30.6 us: one_turn(): lax.all_to_all(messages, ('lat', 'lev'), split_axis=0, concat_axis=0, til...]
    pallas_call x0 -> x6, Pallas kernels: none -> 63.5 us  [the longest x1 23.4 us: to_grid(): pl.pallas_call(grid_kernel, out_shape=(jax.ShapeDtypeStruct((NLON // 2, 1...]
    reshape x5 -> x0, local copies, waits for them, and re-layouts: 42.7 us -> none  [the longest x2 12.5 us: one_sweep(): blocked = field.reshape(shape[0], shape[1], blocks, BLK, shape[3])]
    unnamed x22 -> x14, local copies, waits for them, and re-layouts: 45.3 us -> 2.82 us
    all_to_all x7 -> x0, local copies, waits for them, and re-layouts: 35.7 us -> none  [the longest x1 16.4 us: per_device(): lax.all_to_all(field, 'lat', split_axis=2, concat_axis=3, tiled=True)]
    all_to_all x3 -> x0, other arithmetic: 23.8 us -> none  [the longest x1 15.7 us: per_device(): lax.all_to_all(field, 'lat', split_axis=2, concat_axis=3, tiled=True)]
    transpose x2 -> x0, local copies, waits for them, and re-layouts: 17.4 us -> none  [the longest x1 11.2 us: level_filter(): return jnp.einsum('fkao,faki->fiao', once, lower, precision=precise_mode)]
  transfers between devices with their start and end apart: 4 -> 3, of which waited for: 3 -> 3; matrix products, arithmetic and copies ran while one was open for 6% -> 0% of each run, Pallas kernels for 0% -> 16%
where the time goes in v2:
time: 122 us
  Pallas kernels  63.5 us (52%)
  waiting for transfers between devices  31.7 us (26%)
  starting transfers between devices  22.6 us (19%)
  local copies, waits for them, and re-layouts  2.82 us (2%)
    all_to_all x1, waiting for transfers between devices, one_turn(): lax.all_to_all(messages, ('lat', 'lev'), split_axis=0, concat_axis=0, til...  30.6 us
    pallas_call x1, Pallas kernels, to_grid(): pl.pallas_call(grid_kernel, out_shape=(jax.ShapeDtypeStruct((NLON // 2, 1...  23.4 us
    pallas_call x1, Pallas kernels, make_messages(): pl.pallas_call(send_kernel, out_shape=jax.ShapeDtypeStruct((BANDS, LEVS,...  13.3 us
    all_to_all x1, starting transfers between devices, one_turn(): lax.all_to_all(messages, ('lat', 'lev'), split_axis=0, concat_axis=0, til...  11.5 us
    pallas_call x1, Pallas kernels, smooth_band(): pl.pallas_call(smooth_kernel, grid=(TILES // SHARE,), out_shape=(jax.Shap...  10.1 us
    pallas_call x1, Pallas kernels, add_control(): pl.pallas_call(turn_kernel, grid=(NLON // 128 // WIDE,), out_shape=jax.Sh...  9.16 us
    all_to_all x1, starting transfers between devices, per_device(): lax.all_to_all(joined, 'lat', split_axis=0, concat_axis=0, tiled=True)  7.35 us
    pallas_call x1, Pallas kernels, add_bands(): pl.pallas_call(last_kernel, out_shape=jax.ShapeDtypeStruct(parts.shape, j...  5.54 us
  transfers between devices with their start and end apart: 3, of which 3 were waited for; matrix products, arithmetic and copies ran while one was open for 0% of the time, Pallas kernels for 16%

profile of v2, /device:TPU:1, one launch (start us, length us, event | category | flops | bytes accessed | tf_op | source)
XLA Modules:
  0.0 121.6 jit_solution(6580750375643715091)
XLA Ops:
  0.0 0.0 copy-start.7
  0.0 0.0 copy-start.1
  0.0 0.0 copy-start.2
  0.0 0.0 copy-start.6
  0.0 13.3 %make_messages.2 = f32[32,4,32,128]{3,2,1,0:T(8,128)} custom-call(s32[1]{0:T(128)} %constant.4.clone.1.turn, f32[2048,128]{1,0:T(8,128)} %vals.1, s32[1,2048]{1,0:T(1,128)} %bitcast.21, s32[1,2048]{1,0:T(1,128)} %bitcast.23, f32[128,768]{1,0:T(8,128)} %bitcast.15, f32[4,768]{1,0:T(4,128)} %len_lev.1), custom_call_target="tpu_custom_call" | custom-call | tf_op jit(solution)/shard_map/make_messages/pallas_call | solution.py:217
  13.3 11.5 %all-to-all-start.1 = ((f32[128,32,128]{2,1,0:T(8,128)}), f32[128,32,128]{2,1,0:T(8,128)S(1)}, u32[]{:S(2)}, u32[]{:S(2)}) async-start(f32[128,32,128]{2,1,0:T(8,128)} %bitcast.18), calls=%async_computation.1 | async-start | bytes 4194304 | tf_op jit(solution)/shard_map/all_to_all | solution.py:751
  24.8 30.6 %all-to-all-done.1.recv = f32[128,32,128]{2,1,0:T(8,128)S(1)} async-done(((f32[128,32,128]{2,1,0:T(8,128)}), f32[128,32,128]{2,1,0:T(8,128)S(1)}, u32[]{:S(2)}, u32[]{:S(2)}) %all-to-all-start.1) | async-done | bytes 2097184 | tf_op jit(solution)/shard_map/all_to_all | solution.py:751
  55.4 0.0 copy-start.3
  55.4 1.3 %copy-done.3 = f32[128,32,128]{2,1,0:T(8,128)} copy-done((f32[128,32,128]{2,1,0:T(8,128)}, f32[128,32,128]{2,1,0:T(8,128)S(1)}, u32[]{:S(2)}) %copy-start.3) | copy-done | bytes 2097176
  56.7 0.0 copy-done.7
  56.7 23.4 %to_grid.2 = (f32[768,128]{1,0:T(8,128)}, f32[18432,128]{1,0:T(8,128)}, s32[1]{0:T(128)}) custom-call(f32[128,32,128]{2,1,0:T(8,128)} %copy-done.3, f32[4,8]{1,0:T(4,128)S(1)} %copy-done.7), custom_call_target="tpu_custom_call" | custom-call | tf_op jit(solution)/shard_map/to_grid/pallas_call | solution.py:410
  80.1 0.0 copy-done.1
  80.1 0.0 copy-done.2
  80.2 0.0 copy-done.6
  80.2 0.7 while.12
  80.9 3.8 %all-to-all-start.2 = ((f32[32,24,128]{2,1,0:T(8,128)}), f32[32,24,128]{2,1,0:T(8,128)S(1)}, u32[]{:S(2)}, u32[]{:S(2)}) async-start(f32[32,24,128]{2,1,0:T(8,128)} %bitcast.17), calls=%async_computation.2 | async-start | bytes 786432 | tf_op jit(solution)/shard_map/all_to_all | solution.py:768
  84.6 10.1 %smooth_band.1 = (f32[9216,128]{1,0:T(8,128)}, f32[8,128]{1,0:T(8,128)}) custom-call(f32[18432,128]{1,0:T(8,128)} %get-tuple-element.69.pairs, f32[4,8]{1,0:T(4,128)} %lon_len.5), custom_call_target="tpu_custom_call" | custom-call | flops 20000000 | bytes 14000000 | tf_op jit(solution)/shard_map/smooth_band/pallas_call | solution.py:538
  94.7 0.2 all-to-all-done.2.ends
  94.9 0.0 copy-start.5
  94.9 0.7 copy-done.5
  95.6 2.0 %join_bands.1 = f32[32,24,128]{2,1,0:T(8,128)} custom-call(f32[32,24,128]{2,1,0:T(8,128)} %copy-done.5, f32[4,8]{1,0:T(4,128)S(1)} %get-tuple-element.204, f32[8,128]{1,0:T(8,128)} %get-tuple-element.72._), custom_call_target="tpu_custom_call" | custom-call | tf_op jit(solution)/shard_map/join_bands/pallas_call | solution.py:583
  97.6 7.3 %all-to-all-start.3 = ((f32[32,24,128]{2,1,0:T(8,128)}), f32[32,24,128]{2,1,0:T(8,128)S(1)}, u32[]{:S(2)}, u32[]{:S(2)}) async-start(f32[32,24,128]{2,1,0:T(8,128)} %join_bands.1), calls=%async_computation.3 | async-start | bytes 786432 | tf_op jit(solution)/shard_map/all_to_all | solution.py:771
  105.0 9.2 %add_control.1.parts = f32[4,8,24,1536]{3,2,1,0:T(8,128)} custom-call(f32[6,1536,128]{2,1,0:T(8,128)} %bitcast.19, f32[4,8,24,1536]{3,2,1,0:T(8,128)} %control.1, f32[4,8]{1,0:T(4,128)} %lon_len.5, f32[4,8]{1,0:T(4,128)S(1)} %get-tuple-element.204), custom_call_target="tpu_custom_call" | custom-call | flops 20000000 | bytes 15000000 | tf_op jit(solution)/shard_map/add_control/pallas_call | solution.py:628
  114.1 1.0 all-to-all-done.3
  115.1 0.0 copy-start.4
  115.1 0.7 copy-done.4
  115.9 5.5 %add_bands.1 = f32[4,8,24,1536]{3,2,1,0:T(8,128)} custom-call(f32[4,8]{1,0:T(4,128)S(1)} %get-tuple-element.204, f32[4,8]{1,0:T(4,128)} %lon_len.5, f32[4,8,24,1536]{3,2,1,0:T(8,128)} %add_control.1.parts, f32[768,128]{1,0:T(8,128)} %bitcast.20), custom_call_target="tpu_custom_call" | custom-call | tf_op jit(solution)/shard_map/add_bands/pallas_call | solution.py:725
Async XLA Ops:
  0.0 56.7 %copy-start.7 = (f32[4,8]{1,0:T(4,128)S(1)}, f32[4,8]{1,0:T(4,128)}, u32[]{:S(2)}) copy-start(f32[4,8]{1,0:T(4,128)} %lat_len.7) | copy-start | bytes 388
  0.0 80.1 %copy-start.1 = (f32[2048,128]{1,0:T(8,128)S(1)}, f32[2048,128]{1,0:T(8,128)}, u32[]{:S(2)}) copy-start(f32[2048,128]{1,0:T(8,128)} %vals.1) | copy-start | bytes 3145732
  0.0 80.1 %copy-start.2 = (f32[4,32,768]{2,1,0:T(8,128)S(1)}, f32[4,32,768]{2,1,0:T(8,128)}, u32[]{:S(2)}) copy-start(f32[4,32,768]{2,1,0:T(8,128)} %param.14) | copy-start | bytes 1179652
  0.0 80.1 %copy-start.6 = (f32[4,768]{1,0:T(4,128)S(1)}, f32[4,768]{1,0:T(4,128)}, u32[]{:S(2)}) copy-start(f32[4,768]{1,0:T(4,128)} %len_lev.1) | copy-start | bytes 36868
  13.3 42.1 %all-to-all-start.1 = ((f32[128,32,128]{2,1,0:T(8,128)}), f32[128,32,128]{2,1,0:T(8,128)S(1)}, u32[]{:S(2)}, u32[]{:S(2)}) async-start(f32[128,32,128]{2,1,0:T(8,128)} %bitcast.18), calls=%async_computation.1 | async-start | bytes 4194304 | tf_op jit(solution)/shard_map/all_to_all | solution.py:751
  55.4 1.3 %copy-start.3 = (f32[128,32,128]{2,1,0:T(8,128)}, f32[128,32,128]{2,1,0:T(8,128)S(1)}, u32[]{:S(2)}) copy-start(f32[128,32,128]{2,1,0:T(8,128)S(1)} %all-to-all-done.1.recv) | copy-start | bytes 6291460
  80.9 14.0 %all-to-all-start.2 = ((f32[32,24,128]{2,1,0:T(8,128)}), f32[32,24,128]{2,1,0:T(8,128)S(1)}, u32[]{:S(2)}, u32[]{:S(2)}) async-start(f32[32,24,128]{2,1,0:T(8,128)} %bitcast.17), calls=%async_computation.2 | async-start | bytes 786432 | tf_op jit(solution)/shard_map/all_to_all | solution.py:768
  94.9 0.7 copy-start.5
  97.6 17.5 %all-to-all-start.3 = ((f32[32,24,128]{2,1,0:T(8,128)}), f32[32,24,128]{2,1,0:T(8,128)S(1)}, u32[]{:S(2)}, u32[]{:S(2)}) async-start(f32[32,24,128]{2,1,0:T(8,128)} %join_bands.1), calls=%async_computation.3 | async-start | bytes 786432 | tf_op jit(solution)/shard_map/all_to_all | solution.py:771
  115.1 0.7 copy-start.4

commit v3 on v2

--- a/solution.py
+++ b/solution.py
@@ -23,7 +23,7 @@
 SEGV = 3
 TILES = BAND // GROUP
 PLANE = NLON
-VMEM_LIMIT = 60 * 1024 * 1024
+VMEM_LIMIT = 58 * 1024 * 1024
 PAD = 8
 REGION = BAND // 2 * PLANE
 GRID_ROWS = REGION + PAD
@@ -33,6 +33,7 @@
 BATCH = 2
 SHARE = 2
 WIDE = 4
+UNROLL = 8
 PARTS = 3
 PAIRS = BAND // 2
 
@@ -61,8 +62,12 @@
     return x
 
 
-def send_kernel(turn, vals, owner, column, sigma, len_lev, out, picks, work, lines, xs, places, sem, *place_s):
+def send_kernel(
+    turn, vals_in, owner, column, sigma, len_lev, out, vals, held, heads, picks, work, lines, xs, places, sem, io_sem, *place_s
+):
     rows = vals.shape[0]
+    take = pltpu.make_async_copy(vals_in, vals, io_sem.at[0])
+    take.start()
     tiles = rows // 128
     turn_no = turn[0]
 
@@ -130,7 +135,7 @@
     headers = jnp.where(lane < CAP, headers, 0.0)
     headers = jnp.where(lane == COUNT_LANE, left, headers)
     headers = jnp.where(lane == MOST_LANE, most, headers)
-    headers = jnp.where(lane == SWAP_LANE, swaps, headers)
+    heads[...] = jnp.where(lane == SWAP_LANE, swaps, headers)
 
     sig = sigma[...]
     sig_hi = sig.astype(jnp.bfloat16)
@@ -166,6 +171,7 @@
             lines[at, :] = jnp.transpose(side[128:, :])
         return 0
 
+    take.wait()
     lax.fori_loop(0, rows // width, smooth_levels, 0)
 
     zeros = jnp.zeros((128, 128), jnp.float32)
@@ -192,23 +198,30 @@
     even = (blk & 1) == 0
     lower = blk < 2
 
-    def finish(n, _):
-        done = []
-        for b in (2 * n, 2 * n + 1):
-            x = [xs[pl.ds(pl.multiple_of(q * (BANDS * ROWS) + b * ROWS, ROWS), ROWS), :] for q in range(GROUP)]
-            first = [jnp.where(lower, x[q], pltpu.roll(x[q + 2], 64, 1)) for q in (0, 1)]
-            last = [jnp.where(lower, pltpu.roll(x[q], 64, 1), x[q + 2]) for q in (0, 1)]
-            for l, (u, w) in ((0, first), (2, last)):
-                done.append((b, l, jnp.where(even, u, pltpu.roll(w, 32, 1))))
-                done.append((b, l + 1, jnp.where(even, pltpu.roll(u, 96, 1), w)))
-        for b, l, x in done:
-            out[b, l] = x
-        return 0
-
-    lax.fori_loop(0, BANDS // 2, finish, 0)
-    for b in range(BANDS):
-        for l in range(LEVS):
-            out[b, l, ROWS - 1 : ROWS, :] = headers[b : b + 1]
+    def first_swap(b):
+        x = [xs[pl.ds(pl.multiple_of(q * (BANDS * ROWS) + b * ROWS, ROWS), ROWS), :] for q in range(GROUP)]
+        first = [jnp.where(lower, x[q], pltpu.roll(x[q + 2], 64, 1)) for q in (0, 1)]
+        last = [jnp.where(lower, pltpu.roll(x[q], 64, 1), x[q + 2]) for q in (0, 1)]
+        return first, last
+
+    sends = []
+    for part in range(BANDS // 8):
+        bands = range(part * 8, part * 8 + 8)
+        ahead = first_swap(bands[0])
+        for b in bands:
+            now = ahead
+            if b + 1 in bands:
+                ahead = first_swap(b + 1)
+            for l, (u, w) in ((0, now[0]), (2, now[1])):
+                held[b, l] = jnp.where(even, u, pltpu.roll(w, 32, 1))
+                held[b, l + 1] = jnp.where(even, pltpu.roll(u, 96, 1), w)
+            for l in range(LEVS):
+                held[b, l, ROWS - 1 : ROWS, :] = heads[b : b + 1, :]
+        some = pl.ds(part * 8, 8)
+        sends.append(pltpu.make_async_copy(held.at[some], out.at[some], io_sem.at[1 + part]))
+        sends[-1].start()
+    for copy in sends:
+        copy.wait()
 
 
 def make_messages(turn, vals, owner, column, sigma, len_lev):
@@ -217,15 +230,19 @@
     return pl.pallas_call(
         send_kernel,
         out_shape=jax.ShapeDtypeStruct((BANDS, LEVS, ROWS, 128), jnp.float32),
-        in_specs=[pl.BlockSpec(memory_space=pltpu.SMEM)] + [vmem] * 5,
-        out_specs=vmem,
+        in_specs=[pl.BlockSpec(memory_space=pltpu.SMEM), pl.BlockSpec(memory_space=pltpu.HBM)] + [vmem] * 4,
+        out_specs=pl.BlockSpec(memory_space=pltpu.HBM),
         scratch_shapes=[
+            pltpu.VMEM((rows, 128), jnp.float32),
+            pltpu.VMEM((BANDS, LEVS, ROWS, 128), jnp.float32),
+            pltpu.VMEM((BANDS, 128), jnp.float32),
             pltpu.VMEM((288, NLAT), jnp.bfloat16),
             pltpu.VMEM((2, 256, 128), jnp.float32),
             pltpu.VMEM((rows, 128), jnp.float32),
             pltpu.VMEM((GROUP * BANDS * ROWS, 128), jnp.float32),
             pltpu.VMEM((rows // 64, 128), jnp.int32),
             pltpu.SemaphoreType.DMA((rows // 128,)),
+            pltpu.SemaphoreType.DMA((1 + BANDS // 8,)),
         ]
         + [pltpu.SMEM((1, 128), jnp.int32)] * (rows // 128),
         compiler_params=pltpu.CompilerParams(vmem_limit_bytes=VMEM_LIMIT),
@@ -245,7 +262,7 @@
     return jnp.where(sub < 8 - by, pltpu.roll(x, 8 - by, 0), 0.0)
 
 
-def grid_kernel(recv, lat_len, ends, pairs, most, ga, gb, ups, downs, ids_v, sem, out_sem, *ids_s):
+def grid_kernel(recv, lat_len, ends, grid, most, ga, gb, ups, downs, ids_v, sem, out_sem, *ids_s):
     heads = recv[:, ROWS - 1, :]
     lane = lax.broadcasted_iota(jnp.int32, (128, 128), 1)
     heads = jnp.where(lane == MOST_LANE, jnp.max(heads, axis=0, keepdims=True), heads)
@@ -348,42 +365,51 @@
     def power(n):
         return jnp.broadcast_to(jnp.exp(-im * n.astype(jnp.float32)), (8, 128))
 
-    parity = lane_block & 1
-    to_end = [power(BAND - 1 - 2 * n - parity) for n in range(PAIRS)]
-    to_start = [power(2 * n + parity) for n in range(PAIRS)]
+    to_end = [power(BAND - 1 - 4 * i - lane_block) for i in range(TILES)]
+    to_start = [power(4 * i + lane_block) for i in range(TILES)]
+    blk = blocks_of((8, 128))
+    even = (blk & 1) == 0
+    lower = blk < 2
     out_copies = []
     for part in range(PARTS):
 
         def gather(r, _):
-            row = part * (PLANE // PARTS) + r * 8
-            at = [pl.ds(pl.multiple_of(PAD + n * PLANE + row, 8), 8) for n in range(PAIRS)]
-            cells = [ga[a, :] + gb[a, :] for a in at]
-            up = down = None
-            for n, x in enumerate(cells):
-                up = to_end[n] * x if n == 0 else up + to_end[n] * x
-                down = to_start[n] * x if n == 0 else down + to_start[n] * x
-            for a, x in zip(at, cells):
-                ga[a, :] = x
-            here = pl.ds(pl.multiple_of(row, 8), 8)
-            ups[here, :] = up
-            downs[here, :] = down
+            rows = [part * (PLANE // PARTS) + (r * UNROLL + u) * 8 for u in range(UNROLL)]
+
+            def fold(row):
+                at = [pl.ds(pl.multiple_of(PAD + n * PLANE + row, 8), 8) for n in range(PAIRS)]
+                g = [ga[a, :] + gb[a, :] for a in at]
+                return [fold_lanes(g[2 * i], g[2 * i + 1], lower, 64) for i in range(TILES)]
+
+            def put(row, cells):
+                up = down = None
+                for i, x in enumerate(cells):
+                    up = to_end[i] * x if i == 0 else up + to_end[i] * x
+                    down = to_start[i] * x if i == 0 else down + to_start[i] * x
+                for i, x in enumerate(cells):
+                    ga[pl.ds(pl.multiple_of(PAD + i * PLANE + row, 8), 8), :] = x
+                here = pl.ds(pl.multiple_of(row, 8), 8)
+                ups[here, :] = up
+                downs[here, :] = down
+
+            ahead = [fold(rows[0]), fold(rows[1])]
+            for u, row in enumerate(rows):
+                if u + 2 < UNROLL:
+                    ahead.append(fold(rows[u + 2]))
+                put(row, ahead[u])
             return 0
 
-        lax.fori_loop(0, PLANE // PARTS // 8, gather, 0)
-        for n in range(PAIRS):
-            first = n * PLANE + part * (PLANE // PARTS)
+        lax.fori_loop(0, PLANE // PARTS // 8 // UNROLL, gather, 0)
+        for i in range(TILES):
+            first = i * PLANE + part * (PLANE // PARTS)
             out_copies.append(
                 pltpu.make_async_copy(
                     ga.at[pl.ds(PAD + first, PLANE // PARTS), :],
-                    pairs.at[pl.ds(first, PLANE // PARTS), :],
-                    out_sem.at[part * PAIRS + n],
+                    grid.at[pl.ds(first, PLANE // PARTS), :],
+                    out_sem.at[part * TILES + i],
                 )
             )
             out_copies[-1].start()
-
-    blk = blocks_of((8, 128))
-    even = (blk & 1) == 0
-    lower = blk < 2
 
     def pack(k, _):
         done = []
@@ -411,11 +437,11 @@
         grid_kernel,
         out_shape=(
             jax.ShapeDtypeStruct((NLON // 2, 128), jnp.float32),
-            jax.ShapeDtypeStruct((REGION, 128), jnp.float32),
+            jax.ShapeDtypeStruct((TILES * PLANE, 128), jnp.float32),
             jax.ShapeDtypeStruct((1,), jnp.int32),
         ),
         in_specs=[vmem, smem],
-        out_specs=(vmem, pl.BlockSpec(memory_space=pl.ANY), smem),
+        out_specs=(vmem, pl.BlockSpec(memory_space=pltpu.HBM), smem),
         scratch_shapes=[
             pltpu.VMEM((GRID_ROWS, 128), jnp.float32),
             pltpu.VMEM((GRID_ROWS, 128), jnp.float32),
@@ -423,10 +449,10 @@
             pltpu.VMEM((PLANE, 128), jnp.float32),
             pltpu.VMEM((128, 128), jnp.int32),
             pltpu.SemaphoreType.DMA((ROWS,)),
-            pltpu.SemaphoreType.DMA((PARTS * PAIRS,)),
+            pltpu.SemaphoreType.DMA((PARTS * TILES,)),
         ]
         + [pltpu.SMEM((GROUP, 128), jnp.int32)] * ROWS,
-        compiler_params=pltpu.CompilerParams(vmem_limit_bytes=VMEM_LIMIT),
+        compiler_params=pltpu.CompilerParams(vmem_limit_bytes=32 * 1024 * 1024),
         name="to_grid",
     )(recv, lat_len)
 
@@ -464,13 +490,12 @@
     return (1.0 - one_lon) * (1.0 - one_lon) * ((1.0 - one_lat) / (1.0 + one_lat))
 
 
-def smooth_kernel(pairs, lon_len, local, done, ramp, carry):
+def smooth_kernel(grid, lon_len, local, done, ramp, carry):
     il = 1.0 / in_lanes(lon_len)
     fade = jnp.broadcast_to(jnp.exp(-il), (8, 128))
     stepno = (lax.broadcasted_iota(jnp.int32, (STEP, 128), 0) + 1).astype(jnp.float32)
     ramp[...] = jnp.exp(-stepno * il)
     fades = circle_fades(il)
-    lower = blocks_of((8, 128)) < 2
     vectors = [(i, sv) for i in range(SHARE) for sv in range(SEGV)]
 
     def at_row(i, sv, t):
@@ -479,14 +504,7 @@
     def forward(n, state):
         cells = []
         for u in range(4):
-            cells.append(
-                [
-                    fold_lanes(
-                        pairs[at_row(2 * i, sv, n * 4 + u), :], pairs[at_row(2 * i + 1, sv, n * 4 + u), :], lower, 64
-                    )
-                    for i, sv in vectors
-                ]
-            )
+            cells.append([grid[at_row(i, sv, n * 4 + u), :] for i, sv in vectors])
         for u in range(4):
             state = tuple(fade * y + x for y, x in zip(state, cells[u]))
             cells[u] = state
@@ -534,7 +552,7 @@
     done[...] = fade
 
 
-def smooth_band(pairs, lon_len):
+def smooth_band(grid, lon_len):
     return pl.pallas_call(
         smooth_kernel,
         grid=(TILES // SHARE,),
@@ -543,7 +561,7 @@
             jax.ShapeDtypeStruct((8, 128), jnp.float32),
         ),
         in_specs=[
-            pl.BlockSpec((2 * SHARE * PLANE, 128), lambda n: (n, 0)),
+            pl.BlockSpec((SHARE * PLANE, 128), lambda n: (n, 0)),
             pl.BlockSpec(memory_space=pltpu.SMEM),
         ],
         out_specs=(
@@ -555,9 +573,9 @@
             pltpu.VMEM((SHARE * SEGV, 8, 128), jnp.float32),
         ],
         compiler_params=pltpu.CompilerParams(vmem_limit_bytes=VMEM_LIMIT),
-        cost_estimate=pl.CostEstimate(flops=20_000_000, bytes_accessed=14_000_000, transcendentals=0),
+        cost_estimate=pl.CostEstimate(flops=20_000_000, bytes_accessed=9_400_000, transcendentals=0),
         name="smooth_band",
-    )(pairs, lon_len)
+    )(grid, lon_len)
 
 
 def bands_kernel(ends, lat_len, _, out):
@@ -583,9 +601,9 @@
     return pl.pallas_call(
         bands_kernel,
         out_shape=jax.ShapeDtypeStruct(ends.shape, jnp.float32),
-        in_specs=[vmem, pl.BlockSpec(memory_space=pltpu.SMEM), pl.BlockSpec(memory_space=pl.ANY)],
+        in_specs=[vmem, pl.BlockSpec(memory_space=pltpu.SMEM), pl.BlockSpec(memory_space=pltpu.HBM)],
         out_specs=vmem,
-        compiler_params=pltpu.CompilerParams(vmem_limit_bytes=VMEM_LIMIT),
+        compiler_params=pltpu.CompilerParams(vmem_limit_bytes=8 * 1024 * 1024),
         name="join_bands",
     )(ends, lat_len, after)
 
@@ -721,7 +739,7 @@
 def add_bands(lat_len, lon_len, parts, joined):
     smem = pl.BlockSpec(memory_space=pltpu.SMEM)
     vmem = pl.BlockSpec(memory_space=pltpu.VMEM)
-    hbm = pl.BlockSpec(memory_space=pl.ANY)
+    hbm = pl.BlockSpec(memory_space=pltpu.HBM)
     return pl.pallas_call(
         last_kernel,
         out_shape=jax.ShapeDtypeStruct(parts.shape, jnp.float32),
@@ -736,7 +754,7 @@
             pltpu.VMEM((NLON // 128, PROF, 128), jnp.float32),
             pltpu.SemaphoreType.DMA((2, F * 4)),
         ],
-        compiler_params=pltpu.CompilerParams(vmem_limit_bytes=VMEM_LIMIT),
+        compiler_params=pltpu.CompilerParams(vmem_limit_bytes=32 * 1024 * 1024),
         name="add_bands",
     )(lat_len, lon_len, parts, joined)
 

time: 122 us -> 115 us (0.943)
  Pallas kernels: 63.5 us -> 55 us
  waiting for transfers between devices: 31.7 us -> 35.3 us
  starting transfers between devices: 22.6 us -> 20.4 us
    pallas_call x1, Pallas kernels: 10.1 us -> 6.65 us  [smooth_band(): pl.pallas_call(smooth_kernel, grid=(TILES // SHARE,), out_shape=(jax.Shap...]
    all_to_all x1, starting transfers between devices: 7.35 us -> 3.9 us  [per_device(): lax.all_to_all(joined, 'lat', split_axis=0, concat_axis=0, tiled=True)]
    all_to_all x1, waiting for transfers between devices: 0.16 us -> 3.52 us  [per_device(): ends = lax.all_to_all(ends, 'lat', split_axis=0, concat_axis=0, tiled=True)]
    pallas_call x1, Pallas kernels: 23.4 us -> 20.6 us  [to_grid(): pl.pallas_call(grid_kernel, out_shape=(jax.ShapeDtypeStruct((NLON // 2, 1...]
  transfers between devices with their start and end apart: 3 -> 3, of which waited for: 3 -> 3; matrix products, arithmetic and copies ran while one was open for 0% -> 0% of each run, Pallas kernels for 16% -> 14%
where the time goes in v3:
time: 115 us
  Pallas kernels  55 us (48%)
  waiting for transfers between devices  35.3 us (31%)
  starting transfers between devices  20.4 us (18%)
  local copies, waits for them, and re-layouts  3.03 us (3%)
    all_to_all x1, waiting for transfers between devices, one_turn(): lax.all_to_all(messages, ('lat', 'lev'), split_axis=0, concat_axis=0, til...  30.6 us
    pallas_call x1, Pallas kernels, to_grid(): pl.pallas_call(grid_kernel, out_shape=(jax.ShapeDtypeStruct((NLON // 2, 1...  20.6 us
    pallas_call x1, Pallas kernels, make_messages(): pl.pallas_call(send_kernel, out_shape=jax.ShapeDtypeStruct((BANDS, LEVS,...  12.3 us
    all_to_all x1, starting transfers between devices, one_turn(): lax.all_to_all(messages, ('lat', 'lev'), split_axis=0, concat_axis=0, til...  11.5 us
    pallas_call x1, Pallas kernels, add_control(): pl.pallas_call(turn_kernel, grid=(NLON // 128 // WIDE,), out_shape=jax.Sh...  9.05 us
    pallas_call x1, Pallas kernels, smooth_band(): pl.pallas_call(smooth_kernel, grid=(TILES // SHARE,), out_shape=(jax.Shap...  6.65 us
    all_to_all x1, starting transfers between devices, per_device(): ends = lax.all_to_all(ends, 'lat', split_axis=0, concat_axis=0, tiled=True)  4.96 us
    pallas_call x1, Pallas kernels, add_bands(): pl.pallas_call(last_kernel, out_shape=jax.ShapeDtypeStruct(parts.shape, j...  4.88 us
  transfers between devices with their start and end apart: 3, of which 3 were waited for; matrix products, arithmetic and copies ran while one was open for 0% of the time, Pallas kernels for 14%

profile of v3, /device:TPU:1, one launch (start us, length us, event | category | flops | bytes accessed | tf_op | source)
XLA Modules:
  0.0 114.5 jit_solution(10686979614383769728)
XLA Ops:
  0.0 0.0 copy-start.6
  0.0 0.0 copy-start.3
  0.0 0.0 copy-start.4
  0.0 0.0 copy-start.5
  0.0 12.3 %make_messages.2 = f32[32,4,32,128]{3,2,1,0:T(8,128)} custom-call(s32[1]{0:T(128)} %constant.4.clone.1.turn, f32[2048,128]{1,0:T(8,128)} %vals_in.1, s32[1,2048]{1,0:T(1,128)} %bitcast.21, s32[1,2048]{1,0:T(1,128)} %bitcast.23, f32[128,768]{1,0:T(8,128)} %bitcast.16, f32[4,768]{1,0:T(4,128)} %len_lev.1), custom_call_target="tpu_custom_call" | custom-call | tf_op jit(solution)/shard_map/make_messages/pallas_call | solution.py:230
  12.3 11.5 %all-to-all-start.1 = ((f32[128,32,128]{2,1,0:T(8,128)}), f32[128,32,128]{2,1,0:T(8,128)S(1)}, u32[]{:S(2)}, u32[]{:S(2)}) async-start(f32[128,32,128]{2,1,0:T(8,128)} %bitcast.19), calls=%async_computation.1 | async-start | bytes 4194304 | tf_op jit(solution)/shard_map/all_to_all | solution.py:769
  23.8 30.6 %all-to-all-done.1.recv = f32[128,32,128]{2,1,0:T(8,128)S(1)} async-done(((f32[128,32,128]{2,1,0:T(8,128)}), f32[128,32,128]{2,1,0:T(8,128)S(1)}, u32[]{:S(2)}, u32[]{:S(2)}) %all-to-all-start.1) | async-done | bytes 2097184 | tf_op jit(solution)/shard_map/all_to_all | solution.py:769
  54.4 0.0 copy-done.6
  54.4 20.6 %to_grid.2 = (f32[768,128]{1,0:T(8,128)}, f32[9216,128]{1,0:T(8,128)}, s32[1]{0:T(128)}) custom-call(f32[128,32,128]{2,1,0:T(8,128)S(1)} %all-to-all-done.1.recv, f32[4,8]{1,0:T(4,128)S(1)} %copy-done.6), custom_call_target="tpu_custom_call" | custom-call | tf_op jit(solution)/shard_map/to_grid/pallas_call | solution.py:436
  75.0 0.0 copy-done.3
  75.0 0.0 copy-done.4
  75.0 0.0 copy-done.5
  75.0 0.6 while.12
  75.6 5.0 %all-to-all-start.2 = ((f32[32,24,128]{2,1,0:T(8,128)}), f32[32,24,128]{2,1,0:T(8,128)S(1)}, u32[]{:S(2)}, u32[]{:S(2)}) async-start(f32[32,24,128]{2,1,0:T(8,128)} %bitcast.18), calls=%async_computation.2 | async-start | bytes 786432 | tf_op jit(solution)/shard_map/all_to_all | solution.py:786
  80.6 6.7 %smooth_band.1 = (f32[9216,128]{1,0:T(8,128)}, f32[8,128]{1,0:T(8,128)}) custom-call(f32[9216,128]{1,0:T(8,128)} %get-tuple-element.69.grid, f32[4,8]{1,0:T(4,128)} %lon_len.5), custom_call_target="tpu_custom_call" | custom-call | flops 20000000 | bytes 9400000 | tf_op jit(solution)/shard_map/smooth_band/pallas_call | solution.py:556
  87.2 3.5 %all-to-all-done.2.ends = f32[32,24,128]{2,1,0:T(8,128)S(1)} async-done(((f32[32,24,128]{2,1,0:T(8,128)}), f32[32,24,128]{2,1,0:T(8,128)S(1)}, u32[]{:S(2)}, u32[]{:S(2)}) %all-to-all-start.2) | async-done | bytes 393248 | tf_op jit(solution)/shard_map/all_to_all | solution.py:786
  90.8 0.0 copy-start.2
  90.8 0.7 copy-done.2
  91.4 1.5 %join_bands.1 = f32[32,24,128]{2,1,0:T(8,128)} custom-call(f32[32,24,128]{2,1,0:T(8,128)S(1)} %all-to-all-done.2.ends, f32[4,8]{1,0:T(4,128)S(1)} %get-tuple-element.202, f32[8,128]{1,0:T(8,128)S(1)} %copy-done.2), custom_call_target="tpu_custom_call" | custom-call | tf_op jit(solution)/shard_map/join_bands/pallas_call | solution.py:601
  93.0 3.9 %all-to-all-start.3 = ((f32[32,24,128]{2,1,0:T(8,128)}), f32[32,24,128]{2,1,0:T(8,128)S(1)}, u32[]{:S(2)}, u32[]{:S(2)}) async-start(f32[32,24,128]{2,1,0:T(8,128)} %join_bands.1), calls=%async_computation.3 | async-start | bytes 786432 | tf_op jit(solution)/shard_map/all_to_all | solution.py:789
  96.9 0.0 copy-start.1
  96.9 9.1 %add_control.1.parts = f32[4,8,24,1536]{3,2,1,0:T(8,128)} custom-call(f32[6,1536,128]{2,1,0:T(8,128)} %bitcast.20, f32[4,8,24,1536]{3,2,1,0:T(8,128)} %control.1, f32[4,8]{1,0:T(4,128)} %lon_len.5, f32[4,8]{1,0:T(4,128)S(1)} %get-tuple-element.202), custom_call_target="tpu_custom_call" | custom-call | flops 20000000 | bytes 15000000 | tf_op jit(solution)/shard_map/add_control/pallas_call | solution.py:646
  105.9 1.2 %all-to-all-done.3 = f32[32,24,128]{2,1,0:T(8,128)S(1)} async-done(((f32[32,24,128]{2,1,0:T(8,128)}), f32[32,24,128]{2,1,0:T(8,128)S(1)}, u32[]{:S(2)}, u32[]{:S(2)}) %all-to-all-start.3) | async-done | bytes 393248 | tf_op jit(solution)/shard_map/all_to_all | solution.py:789
  107.2 0.0 copy-done.1
  107.2 0.0 copy-start
  107.2 2.3 %copy-done = f32[4,8,24,1536]{3,2,1,0:T(8,128)S(1)} copy-done((f32[4,8,24,1536]{3,2,1,0:T(8,128)S(1)}, f32[4,8,24,1536]{3,2,1,0:T(8,128)}, u32[]{:S(2)}) %copy-start) | copy-done | bytes 4718616
  109.5 4.9 %add_bands.1 = f32[4,8,24,1536]{3,2,1,0:T(8,128)} custom-call(f32[4,8]{1,0:T(4,128)S(1)} %get-tuple-element.202, f32[4,8]{1,0:T(4,128)S(1)} %copy-done.1, f32[4,8,24,1536]{3,2,1,0:T(8,128)S(1)} %copy-done, f32[768,128]{1,0:T(8,128)S(1)} %bitcast.14), custom_call_target="tpu_custom_call" | custom-call | tf_op jit(solution)/shard_map/add_bands/pallas_call | solution.py:743
Async XLA Ops:
  0.0 54.4 %copy-start.6 = (f32[4,8]{1,0:T(4,128)S(1)}, f32[4,8]{1,0:T(4,128)}, u32[]{:S(2)}) copy-start(f32[4,8]{1,0:T(4,128)} %lat_len.7) | copy-start | bytes 388
  0.0 75.0 %copy-start.3 = (f32[2048,128]{1,0:T(8,128)S(1)}, f32[2048,128]{1,0:T(8,128)}, u32[]{:S(2)}) copy-start(f32[2048,128]{1,0:T(8,128)} %vals_in.1) | copy-start | bytes 3145732
  0.0 75.0 %copy-start.4 = (f32[4,32,768]{2,1,0:T(8,128)S(1)}, f32[4,32,768]{2,1,0:T(8,128)}, u32[]{:S(2)}) copy-start(f32[4,32,768]{2,1,0:T(8,128)} %param.14) | copy-start | bytes 1179652
  0.0 75.0 %copy-start.5 = (f32[4,768]{1,0:T(4,128)S(1)}, f32[4,768]{1,0:T(4,128)}, u32[]{:S(2)}) copy-start(f32[4,768]{1,0:T(4,128)} %len_lev.1) | copy-start | bytes 36868
  12.3 42.1 %all-to-all-start.1 = ((f32[128,32,128]{2,1,0:T(8,128)}), f32[128,32,128]{2,1,0:T(8,128)S(1)}, u32[]{:S(2)}, u32[]{:S(2)}) async-start(f32[128,32,128]{2,1,0:T(8,128)} %bitcast.19), calls=%async_computation.1 | async-start | bytes 4194304 | tf_op jit(solution)/shard_map/all_to_all | solution.py:769
  75.6 15.1 %all-to-all-start.2 = ((f32[32,24,128]{2,1,0:T(8,128)}), f32[32,24,128]{2,1,0:T(8,128)S(1)}, u32[]{:S(2)}, u32[]{:S(2)}) async-start(f32[32,24,128]{2,1,0:T(8,128)} %bitcast.18), calls=%async_computation.2 | async-start | bytes 786432 | tf_op jit(solution)/shard_map/all_to_all | solution.py:786
  90.8 0.7 copy-start.2
  93.0 14.2 %all-to-all-start.3 = ((f32[32,24,128]{2,1,0:T(8,128)}), f32[32,24,128]{2,1,0:T(8,128)S(1)}, u32[]{:S(2)}, u32[]{:S(2)}) async-start(f32[32,24,128]{2,1,0:T(8,128)} %join_bands.1), calls=%async_computation.3 | async-start | bytes 786432 | tf_op jit(solution)/shard_map/all_to_all | solution.py:789
  96.9 10.3 %copy-start.1 = (f32[4,8]{1,0:T(4,128)S(1)}, f32[4,8]{1,0:T(4,128)}, u32[]{:S(2)}) copy-start(f32[4,8]{1,0:T(4,128)} %lon_len.5) | copy-start | bytes 388
  107.2 2.3 %copy-start = (f32[4,8,24,1536]{3,2,1,0:T(8,128)S(1)}, f32[4,8,24,1536]{3,2,1,0:T(8,128)}, u32[]{:S(2)}) copy-start(f32[4,8,24,1536]{3,2,1,0:T(8,128)} %add_control.1.parts) | copy-start | bytes 14155780

commit v4 on v3

--- a/solution.py
+++ b/solution.py
@@ -30,10 +30,11 @@
 HALF_CAP = CAP // 2
 SWAP_LANE = 126
 SAME_LANE = 127
-BATCH = 2
+BATCH = 3
 SHARE = 2
 WIDE = 4
 UNROLL = 8
+FIRST, NEXT = 18, 6
 PARTS = 3
 PAIRS = BAND // 2
 
@@ -63,8 +64,10 @@
 
 
 def send_kernel(
-    turn, vals_in, owner, column, sigma, len_lev, out, vals, held, heads, picks, work, lines, xs, places, sem, io_sem, *place_s
+    turn, vals_in, owner, column, sigma, len_lev, out, vals, held, heads, picks, lines, xs, places, sem, io_sem, *more
 ):
+    stage_a, stage_b, work_a, work_b, fades_a, fades_b = more[:6]
+    place_s = more[6:]
     rows = vals.shape[0]
     take = pltpu.make_async_copy(vals_in, vals, io_sem.at[0])
     take.start()
@@ -135,7 +138,11 @@
     headers = jnp.where(lane < CAP, headers, 0.0)
     headers = jnp.where(lane == COUNT_LANE, left, headers)
     headers = jnp.where(lane == MOST_LANE, most, headers)
-    heads[...] = jnp.where(lane == SWAP_LANE, swaps, headers)
+    headers = jnp.where(lane == SWAP_LANE, swaps, headers)
+    heads[0] = headers
+    place_no = jnp.where(lane < CAP, lane & 3, 1)
+    headers = jnp.where(place_no == 2, pltpu.roll(headers, 2, 1), jnp.where(place_no == 0, pltpu.roll(headers, 126, 1), headers))
+    heads[1] = headers
 
     sig = sigma[...]
     sig_hi = sig.astype(jnp.bfloat16)
@@ -149,30 +156,42 @@
     picks[256:288, :] = jnp.concatenate([f_hi, f_mid, f_lo, jnp.zeros_like(fade)], axis=0).astype(jnp.bfloat16)
     lat_id = lax.broadcasted_iota(jnp.int32, (NLAT, width), 0)
 
-    def smooth_levels(k, _):
+    def pick(k, stage, fades):
         which = jnp.concatenate([places[pl.ds(tiles + 2 * k + g, 1), :] for g in (0, 1)], axis=1)
         at_lat = jnp.where(lat_id == which, 1.0, 0.0).astype(jnp.bfloat16)
         got = jnp.dot(picks[...], at_lat, preferred_element_type=jnp.float32)
         for g in (0, 1):
             lanes = slice(g * 128, (g + 1) * 128)
             at = pl.ds(pl.multiple_of(k * width + g * 128, 128), 128)
+            stage[g] = jnp.transpose(vals[at, :]) * (got[0:128, lanes] + got[128:256, lanes])
+        fades[...] = got[256:264, :] + got[264:272, :] + got[272:280, :]
+
+    def smooth_levels(k, stage, fades, work):
+        for g in (0, 1):
             side = work.at[g]
-            side[0:128, :] = jnp.transpose(vals[at, :]) * (got[0:128, lanes] + got[128:256, lanes])
-            a = got[256:260, lanes] + got[264:268, lanes] + got[272:276, lanes]
-            y = [side[pl.ds(0, F, stride=NLEV), :]]
+            a = fades[0:F, g * 128 : (g + 1) * 128]
+            y = [stage[g, pl.ds(0, F, stride=NLEV), :]]
             for n in range(1, NLEV):
-                y.append(a * y[-1] + side[pl.ds(n, F, stride=NLEV), :])
+                y.append(a * y[-1] + stage[g, pl.ds(n, F, stride=NLEV), :])
             gain = (1.0 - a) * (1.0 - a)
             w = y[-1]
             for n in range(NLEV - 1, -1, -1):
                 if n < NLEV - 1:
                     w = a * w + y[n]
-                side[pl.ds(128 + n // LEVQ * PROF + n % LEVQ, F, stride=LEVQ), :] = w * gain
-            lines[at, :] = jnp.transpose(side[128:, :])
+                side[pl.ds(n // LEVQ * PROF + n % LEVQ, F, stride=LEVQ), :] = w * gain
+        for g in (0, 1):
+            lines[pl.ds(pl.multiple_of(k * width + g * 128, 128), 128), :] = jnp.transpose(work[g])
+
+    def two_blocks(n, _):
+        pick(2 * n + 1, stage_b, fades_b)
+        smooth_levels(2 * n, stage_a, fades_a, work_a)
+        pick(jnp.minimum(2 * n + 2, rows // width - 1), stage_a, fades_a)
+        smooth_levels(2 * n + 1, stage_b, fades_b, work_b)
         return 0
 
     take.wait()
-    lax.fori_loop(0, rows // width, smooth_levels, 0)
+    pick(0, stage_a, fades_a)
+    lax.fori_loop(0, rows // width // 2, two_blocks, 0)
 
     zeros = jnp.zeros((128, 128), jnp.float32)
 
@@ -198,11 +217,14 @@
     even = (blk & 1) == 0
     lower = blk < 2
 
+    def swap(a, b, keep, by):
+        turned = pltpu.roll(jnp.where(keep, b, a), by, 1)
+        return jnp.where(keep, a, turned), jnp.where(keep, turned, b)
+
     def first_swap(b):
         x = [xs[pl.ds(pl.multiple_of(q * (BANDS * ROWS) + b * ROWS, ROWS), ROWS), :] for q in range(GROUP)]
-        first = [jnp.where(lower, x[q], pltpu.roll(x[q + 2], 64, 1)) for q in (0, 1)]
-        last = [jnp.where(lower, pltpu.roll(x[q], 64, 1), x[q + 2]) for q in (0, 1)]
-        return first, last
+        pairs = [swap(x[q], x[q + 2], lower, 64) for q in (0, 1)]
+        return [p[0] for p in pairs], [p[1] for p in pairs]
 
     sends = []
     for part in range(BANDS // 8):
@@ -213,10 +235,9 @@
             if b + 1 in bands:
                 ahead = first_swap(b + 1)
             for l, (u, w) in ((0, now[0]), (2, now[1])):
-                held[b, l] = jnp.where(even, u, pltpu.roll(w, 32, 1))
-                held[b, l + 1] = jnp.where(even, pltpu.roll(u, 96, 1), w)
+                held[b, l], held[b, l + 1] = swap(u, w, even, 32)
             for l in range(LEVS):
-                held[b, l, ROWS - 1 : ROWS, :] = heads[b : b + 1, :]
+                held[b, l, ROWS - 1 : ROWS, :] = heads[l % 2, b : b + 1, :]
         some = pl.ds(part * 8, 8)
         sends.append(pltpu.make_async_copy(held.at[some], out.at[some], io_sem.at[1 + part]))
         sends[-1].start()
@@ -235,15 +256,16 @@
         scratch_shapes=[
             pltpu.VMEM((rows, 128), jnp.float32),
             pltpu.VMEM((BANDS, LEVS, ROWS, 128), jnp.float32),
-            pltpu.VMEM((BANDS, 128), jnp.float32),
+            pltpu.VMEM((2, BANDS, 128), jnp.float32),
             pltpu.VMEM((288, NLAT), jnp.bfloat16),
-            pltpu.VMEM((2, 256, 128), jnp.float32),
             pltpu.VMEM((rows, 128), jnp.float32),
             pltpu.VMEM((GROUP * BANDS * ROWS, 128), jnp.float32),
             pltpu.VMEM((rows // 64, 128), jnp.int32),
             pltpu.SemaphoreType.DMA((rows // 128,)),
             pltpu.SemaphoreType.DMA((1 + BANDS // 8,)),
         ]
+        + [pltpu.VMEM((2, 128, 128), jnp.float32)] * 4
+        + [pltpu.VMEM((8, 256), jnp.float32)] * 2
         + [pltpu.SMEM((1, 128), jnp.int32)] * (rows // 128),
         compiler_params=pltpu.CompilerParams(vmem_limit_bytes=VMEM_LIMIT),
         name="make_messages",
@@ -268,11 +290,13 @@
     heads = jnp.where(lane == MOST_LANE, jnp.max(heads, axis=0, keepdims=True), heads)
     ids = jnp.transpose(heads).astype(jnp.int32)
     same = jnp.zeros((8, 128), jnp.bool_)
-    for m in range(0, 128, 16):
-        a, b = ids[m : m + 8], ids[m + 8 : m + 16]
-        turned = pltpu.roll(b, 4, 0)
-        same = same | ((a >= PAD) & ((a == pltpu.roll(a, 4, 0)) | (a == b) | (a == turned)))
-        same = same | ((b >= PAD) & (b == turned))
+    for m in range(0, 128, 8):
+        a = ids[m : m + 8]
+        again = a == pltpu.roll(a, 4, 0)
+        if m < 120:
+            b = ids[m + 8 : m + 16]
+            again = again | (a == b) | (a == pltpu.roll(b, 4, 0))
+        same = same | ((a >= PAD) & again)
     same = jnp.max(jnp.where(same, 1, 0), axis=0, keepdims=True)
     ids_v[...] = ids
     ids_v[SAME_LANE : SAME_LANE + 1, :] = same
@@ -325,12 +349,12 @@
                         pltpu.store(g.at[at[m][q], :], held[m][q] + row[m], mask=masks[q])
 
         def add_message(batch):
-            add_rows(0, 12, batch)
-            for lo in range(12, ROWS - 1, 4):
+            add_rows(0, FIRST, batch)
+            for lo in range(FIRST, ROWS - 1, NEXT):
 
                 @pl.when(n > GROUP * lo)
                 def _():
-                    add_rows(lo, min(lo + 4, ROWS - 1), batch)
+                    add_rows(lo, min(lo + NEXT, ROWS - 1), batch)
 
         @pl.when(swaps + sames == 0)
         def _():
@@ -491,6 +515,7 @@
 
 
 def smooth_kernel(grid, lon_len, local, done, ramp, carry):
+    done[0] = 1
     il = 1.0 / in_lanes(lon_len)
     fade = jnp.broadcast_to(jnp.exp(-il), (8, 128))
     stepno = (lax.broadcasted_iota(jnp.int32, (STEP, 128), 0) + 1).astype(jnp.float32)
@@ -549,7 +574,6 @@
         return 0
 
     lax.fori_loop(0, STEP // 4, finish, 0)
-    done[...] = fade
 
 
 def smooth_band(grid, lon_len):
@@ -558,7 +582,7 @@
         grid=(TILES // SHARE,),
         out_shape=(
             jax.ShapeDtypeStruct((TILES * PLANE, 128), jnp.float32),
-            jax.ShapeDtypeStruct((8, 128), jnp.float32),
+            jax.ShapeDtypeStruct((1,), jnp.int32),
         ),
         in_specs=[
             pl.BlockSpec((SHARE * PLANE, 128), lambda n: (n, 0)),
@@ -566,7 +590,7 @@
         ],
         out_specs=(
             pl.BlockSpec((SHARE * PLANE, 128), lambda n: (n, 0)),
-            pl.BlockSpec(memory_space=pltpu.VMEM),
+            pl.BlockSpec(memory_space=pltpu.SMEM),
         ),
         scratch_shapes=[
             pltpu.VMEM((STEP, 128), jnp.float32),
@@ -601,7 +625,7 @@
     return pl.pallas_call(
         bands_kernel,
         out_shape=jax.ShapeDtypeStruct(ends.shape, jnp.float32),
-        in_specs=[vmem, pl.BlockSpec(memory_space=pltpu.SMEM), pl.BlockSpec(memory_space=pltpu.HBM)],
+        in_specs=[vmem] + [pl.BlockSpec(memory_space=pltpu.SMEM)] * 2,
         out_specs=vmem,
         compiler_params=pltpu.CompilerParams(vmem_limit_bytes=8 * 1024 * 1024),
         name="join_bands",
@@ -754,7 +778,8 @@
             pltpu.VMEM((NLON // 128, PROF, 128), jnp.float32),
             pltpu.SemaphoreType.DMA((2, F * 4)),
         ],
-        compiler_params=pltpu.CompilerParams(vmem_limit_bytes=32 * 1024 * 1024),
+        compiler_params=pltpu.CompilerParams(vmem_limit_bytes=24 * 1024 * 1024),
+        input_output_aliases={2: 0},
         name="add_bands",
     )(lat_len, lon_len, parts, joined)
 

time: 115 us -> 111 us (0.965)
  local copies, waits for them, and re-layouts: 3.03 us -> 0.02 us
  Pallas kernels: 55 us -> 52.6 us
    unnamed x14 -> x10, local copies, waits for them, and re-layouts: 3.03 us -> 0.02 us
    pallas_call x1, Pallas kernels: 20.6 us -> 18.3 us  [to_grid(): pl.pallas_call(grid_kernel, out_shape=(jax.ShapeDtypeStruct((NLON // 2, 1...]
where the time goes in v4:
time: 111 us; the launch traced here: 109 us
  Pallas kernels  52.6 us (47%)
  waiting for transfers between devices  35.3 us (32%)
  starting transfers between devices  20.4 us (18%)
    all_to_all x1, waiting for transfers between devices, one_turn(): lax.all_to_all(messages, ('lat', 'lev'), split_axis=0, concat_axis=0, til...  30.6 us
    pallas_call x1, Pallas kernels, to_grid(): pl.pallas_call(grid_kernel, out_shape=(jax.ShapeDtypeStruct((NLON // 2, 1...  18.3 us
    all_to_all x1, starting transfers between devices, one_turn(): lax.all_to_all(messages, ('lat', 'lev'), split_axis=0, concat_axis=0, til...  11.5 us
    pallas_call x1, Pallas kernels, make_messages(): pl.pallas_call(send_kernel, out_shape=jax.ShapeDtypeStruct((BANDS, LEVS,...  11.3 us
    pallas_call x1, Pallas kernels, add_control(): pl.pallas_call(turn_kernel, grid=(NLON // 128 // WIDE,), out_shape=jax.Sh...  9.05 us
    pallas_call x1, Pallas kernels, smooth_band(): pl.pallas_call(smooth_kernel, grid=(TILES // SHARE,), out_shape=(jax.Shap...  6.62 us
    pallas_call x1, Pallas kernels, add_bands(): pl.pallas_call(last_kernel, out_shape=jax.ShapeDtypeStruct(parts.shape, j...  5.13 us
    all_to_all x1, starting transfers between devices, per_device(): ends = lax.all_to_all(ends, 'lat', split_axis=0, concat_axis=0, tiled=True)  5.03 us
  transfers between devices with their start and end apart: 3, of which 3 were waited for; matrix products, arithmetic and copies ran while one was open for 0% of the time, Pallas kernels for 14%

profile of v4, /device:TPU:1, one launch (start us, length us, event | category | flops | bytes accessed | tf_op | source)
XLA Modules:
  0.0 109.5 jit_solution(7211079252728613410)
XLA Ops:
  0.0 0.0 copy-start.4
  0.0 0.0 copy-start.1
  0.0 0.0 copy-start.2
  0.0 0.0 copy-start.3
  0.0 11.3 %make_messages.2 = f32[32,4,32,128]{3,2,1,0:T(8,128)} custom-call(s32[1]{0:T(128)} %constant.4.clone.1.turn, f32[2048,128]{1,0:T(8,128)} %vals_in.1, s32[1,2048]{1,0:T(1,128)} %bitcast.21, s32[1,2048]{1,0:T(1,128)} %bitcast.23, f32[128,768]{1,0:T(8,128)} %bitcast.16, f32[4,768]{1,0:T(4,128)} %len_lev.1), custom_call_target="tpu_custom_call" | custom-call | tf_op jit(solution)/shard_map/make_messages/pallas_call | solution.py:251
  11.3 11.5 %all-to-all-start.1 = ((f32[128,32,128]{2,1,0:T(8,128)}), f32[128,32,128]{2,1,0:T(8,128)S(1)}, u32[]{:S(2)}, u32[]{:S(2)}) async-start(f32[128,32,128]{2,1,0:T(8,128)} %bitcast.19), calls=%async_computation.1 | async-start | bytes 4194304 | tf_op jit(solution)/shard_map/all_to_all | solution.py:794
  22.8 30.6 %all-to-all-done.1.recv = f32[128,32,128]{2,1,0:T(8,128)S(1)} async-done(((f32[128,32,128]{2,1,0:T(8,128)}), f32[128,32,128]{2,1,0:T(8,128)S(1)}, u32[]{:S(2)}, u32[]{:S(2)}) %all-to-all-start.1) | async-done | bytes 2097184 | tf_op jit(solution)/shard_map/all_to_all | solution.py:794
  53.4 0.0 copy-done.4
  53.4 18.3 %to_grid.2 = (f32[768,128]{1,0:T(8,128)}, f32[9216,128]{1,0:T(8,128)}, s32[1]{0:T(128)}) custom-call(f32[128,32,128]{2,1,0:T(8,128)S(1)} %all-to-all-done.1.recv, f32[4,8]{1,0:T(4,128)S(1)} %copy-done.4), custom_call_target="tpu_custom_call" | custom-call | tf_op jit(solution)/shard_map/to_grid/pallas_call | solution.py:460
  71.7 0.0 copy-done.1
  71.7 0.0 copy-done.2
  71.7 0.0 copy-done.3
  71.7 0.8 while.12
  72.5 5.0 %all-to-all-start.2 = ((f32[32,24,128]{2,1,0:T(8,128)}), f32[32,24,128]{2,1,0:T(8,128)S(1)}, u32[]{:S(2)}, u32[]{:S(2)}) async-start(f32[32,24,128]{2,1,0:T(8,128)} %bitcast.18), calls=%async_computation.2 | async-start | bytes 786432 | tf_op jit(solution)/shard_map/all_to_all | solution.py:811
  77.6 6.6 %smooth_band.1 = (f32[9216,128]{1,0:T(8,128)}, s32[1]{0:T(128)}) custom-call(f32[9216,128]{1,0:T(8,128)} %get-tuple-element.69.grid, f32[4,8]{1,0:T(4,128)} %lon_len.5), custom_call_target="tpu_custom_call" | custom-call | flops 20000000 | bytes 9400000 | tf_op jit(solution)/shard_map/smooth_band/pallas_call | solution.py:580
  84.2 3.5 %all-to-all-done.2.ends = f32[32,24,128]{2,1,0:T(8,128)S(1)} async-done(((f32[32,24,128]{2,1,0:T(8,128)}), f32[32,24,128]{2,1,0:T(8,128)S(1)}, u32[]{:S(2)}, u32[]{:S(2)}) %all-to-all-start.2) | async-done | bytes 393248 | tf_op jit(solution)/shard_map/all_to_all | solution.py:811
  87.8 2.2 %join_bands.1 = f32[32,24,128]{2,1,0:T(8,128)} custom-call(f32[32,24,128]{2,1,0:T(8,128)S(1)} %all-to-all-done.2.ends, f32[4,8]{1,0:T(4,128)S(1)} %get-tuple-element.202, s32[1]{0:T(128)} %get-tuple-element.72._), custom_call_target="tpu_custom_call" | custom-call | tf_op jit(solution)/shard_map/join_bands/pallas_call | solution.py:625
  90.0 3.9 %all-to-all-start.3 = ((f32[32,24,128]{2,1,0:T(8,128)}), f32[32,24,128]{2,1,0:T(8,128)S(1)}, u32[]{:S(2)}, u32[]{:S(2)}) async-start(f32[32,24,128]{2,1,0:T(8,128)} %join_bands.1), calls=%async_computation.3 | async-start | bytes 786432 | tf_op jit(solution)/shard_map/all_to_all | solution.py:814
  93.9 0.0 copy-start
  93.9 9.1 %add_control.1.parts = f32[4,8,24,1536]{3,2,1,0:T(8,128)} custom-call(f32[6,1536,128]{2,1,0:T(8,128)} %bitcast.20, f32[4,8,24,1536]{3,2,1,0:T(8,128)} %control.1, f32[4,8]{1,0:T(4,128)} %lon_len.5, f32[4,8]{1,0:T(4,128)S(1)} %get-tuple-element.202), custom_call_target="tpu_custom_call" | custom-call | flops 20000000 | bytes 15000000 | tf_op jit(solution)/shard_map/add_control/pallas_call | solution.py:670
  102.9 1.2 %all-to-all-done.3 = f32[32,24,128]{2,1,0:T(8,128)S(1)} async-done(((f32[32,24,128]{2,1,0:T(8,128)}), f32[32,24,128]{2,1,0:T(8,128)S(1)}, u32[]{:S(2)}, u32[]{:S(2)}) %all-to-all-start.3) | async-done | bytes 393248 | tf_op jit(solution)/shard_map/all_to_all | solution.py:814
  104.2 0.0 copy-done
  104.2 5.1 %add_bands.1 = f32[4,8,24,1536]{3,2,1,0:T(8,128)} custom-call(f32[4,8]{1,0:T(4,128)S(1)} %get-tuple-element.202, f32[4,8]{1,0:T(4,128)S(1)} %copy-done, f32[4,8,24,1536]{3,2,1,0:T(8,128)} %add_control.1.parts, f32[768,128]{1,0:T(8,128)S(1)} %bitcast.14), custom_call_target="tpu_custom_call", output_to_operand_aliasing={{}: (2, {})} | custom-call | tf_op jit(solution)/shard_map/add_bands/pallas_call | solution.py:767
Async XLA Ops:
  0.0 53.4 %copy-start.4 = (f32[4,8]{1,0:T(4,128)S(1)}, f32[4,8]{1,0:T(4,128)}, u32[]{:S(2)}) copy-start(f32[4,8]{1,0:T(4,128)} %lat_len.7) | copy-start | bytes 388
  0.0 71.7 %copy-start.1 = (f32[2048,128]{1,0:T(8,128)S(1)}, f32[2048,128]{1,0:T(8,128)}, u32[]{:S(2)}) copy-start(f32[2048,128]{1,0:T(8,128)} %vals_in.1) | copy-start | bytes 3145732
  0.0 71.7 %copy-start.2 = (f32[4,32,768]{2,1,0:T(8,128)S(1)}, f32[4,32,768]{2,1,0:T(8,128)}, u32[]{:S(2)}) copy-start(f32[4,32,768]{2,1,0:T(8,128)} %param.14) | copy-start | bytes 1179652
  0.0 71.7 %copy-start.3 = (f32[4,768]{1,0:T(4,128)S(1)}, f32[4,768]{1,0:T(4,128)}, u32[]{:S(2)}) copy-start(f32[4,768]{1,0:T(4,128)} %len_lev.1) | copy-start | bytes 36868
  11.3 42.1 %all-to-all-start.1 = ((f32[128,32,128]{2,1,0:T(8,128)}), f32[128,32,128]{2,1,0:T(8,128)S(1)}, u32[]{:S(2)}, u32[]{:S(2)}) async-start(f32[128,32,128]{2,1,0:T(8,128)} %bitcast.19), calls=%async_computation.1 | async-start | bytes 4194304 | tf_op jit(solution)/shard_map/all_to_all | solution.py:794
  72.5 15.2 %all-to-all-start.2 = ((f32[32,24,128]{2,1,0:T(8,128)}), f32[32,24,128]{2,1,0:T(8,128)S(1)}, u32[]{:S(2)}, u32[]{:S(2)}) async-start(f32[32,24,128]{2,1,0:T(8,128)} %bitcast.18), calls=%async_computation.2 | async-start | bytes 786432 | tf_op jit(solution)/shard_map/all_to_all | solution.py:811
  90.0 14.2 %all-to-all-start.3 = ((f32[32,24,128]{2,1,0:T(8,128)}), f32[32,24,128]{2,1,0:T(8,128)S(1)}, u32[]{:S(2)}, u32[]{:S(2)}) async-start(f32[32,24,128]{2,1,0:T(8,128)} %join_bands.1), calls=%async_computation.3 | async-start | bytes 786432 | tf_op jit(solution)/shard_map/all_to_all | solution.py:814
  93.9 10.3 %copy-start = (f32[4,8]{1,0:T(4,128)S(1)}, f32[4,8]{1,0:T(4,128)}, u32[]{:S(2)}) copy-start(f32[4,8]{1,0:T(4,128)} %lon_len.5) | copy-start | bytes 388

commit v5 on v4

--- a/solution.py
+++ b/solution.py
@@ -33,7 +33,7 @@
 BATCH = 3
 SHARE = 2
 WIDE = 4
-UNROLL = 8
+UNROLL = 16
 FIRST, NEXT = 18, 6
 PARTS = 3
 PAIRS = BAND // 2
@@ -64,13 +64,15 @@
 
 
 def send_kernel(
-    turn, vals_in, owner, column, sigma, len_lev, out, vals, held, heads, picks, lines, xs, places, sem, io_sem, *more
+    turn, vals_in, owner, column, sigma_in, len_lev, out, vals, sigma, held, heads, picks, lines, xs, places, sem, io_sem, *more
 ):
     stage_a, stage_b, work_a, work_b, fades_a, fades_b = more[:6]
     place_s = more[6:]
     rows = vals.shape[0]
     take = pltpu.make_async_copy(vals_in, vals, io_sem.at[0])
     take.start()
+    take_sigma = pltpu.make_async_copy(sigma_in, sigma, io_sem.at[1 + BANDS // 8])
+    take_sigma.start()
     tiles = rows // 128
     turn_no = turn[0]
 
@@ -144,6 +146,7 @@
     headers = jnp.where(place_no == 2, pltpu.roll(headers, 2, 1), jnp.where(place_no == 0, pltpu.roll(headers, 126, 1), headers))
     heads[1] = headers
 
+    take_sigma.wait()
     sig = sigma[...]
     sig_hi = sig.astype(jnp.bfloat16)
     picks[0:128, :] = sig_hi
@@ -248,13 +251,15 @@
 def make_messages(turn, vals, owner, column, sigma, len_lev):
     rows = vals.shape[0]
     vmem = pl.BlockSpec(memory_space=pltpu.VMEM)
+    hbm = pl.BlockSpec(memory_space=pltpu.HBM)
     return pl.pallas_call(
         send_kernel,
         out_shape=jax.ShapeDtypeStruct((BANDS, LEVS, ROWS, 128), jnp.float32),
-        in_specs=[pl.BlockSpec(memory_space=pltpu.SMEM), pl.BlockSpec(memory_space=pltpu.HBM)] + [vmem] * 4,
+        in_specs=[pl.BlockSpec(memory_space=pltpu.SMEM), hbm, vmem, vmem, hbm, vmem],
         out_specs=pl.BlockSpec(memory_space=pltpu.HBM),
         scratch_shapes=[
             pltpu.VMEM((rows, 128), jnp.float32),
+            pltpu.VMEM((F * NLEV, NLAT), jnp.float32),
             pltpu.VMEM((BANDS, LEVS, ROWS, 128), jnp.float32),
             pltpu.VMEM((2, BANDS, 128), jnp.float32),
             pltpu.VMEM((288, NLAT), jnp.bfloat16),
@@ -262,7 +267,7 @@
             pltpu.VMEM((GROUP * BANDS * ROWS, 128), jnp.float32),
             pltpu.VMEM((rows // 64, 128), jnp.int32),
             pltpu.SemaphoreType.DMA((rows // 128,)),
-            pltpu.SemaphoreType.DMA((1 + BANDS // 8,)),
+            pltpu.SemaphoreType.DMA((2 + BANDS // 8,)),
         ]
         + [pltpu.VMEM((2, 128, 128), jnp.float32)] * 4
         + [pltpu.VMEM((8, 256), jnp.float32)] * 2
@@ -299,7 +304,10 @@
         same = same | ((a >= PAD) & again)
     same = jnp.max(jnp.where(same, 1, 0), axis=0, keepdims=True)
     ids_v[...] = ids
-    ids_v[SAME_LANE : SAME_LANE + 1, :] = same
+    count = ids[COUNT_LANE : COUNT_LANE + 1, :]
+    ids_v[COUNT_LANE : COUNT_LANE + 1, :] = jnp.maximum(count, pltpu.roll(count, 64, 1))
+    care = same + 2 * ids[SWAP_LANE : SWAP_LANE + 1, :]
+    ids_v[SAME_LANE : SAME_LANE + 1, :] = jnp.maximum(care, pltpu.roll(care, 64, 1))
     copies = [
         pltpu.make_async_copy(ids_v.at[pl.ds(GROUP * j, GROUP), :], ids_s[j], sem.at[j]) for j in range(ROWS)
     ]
@@ -327,9 +335,8 @@
 
     def add_source(s, _):
         pair = ((s, ga), (s + half, gb))
-        n = jnp.maximum(tail[COUNT_LANE - CAP, s], tail[COUNT_LANE - CAP, s + half])
-        swaps = tail[SWAP_LANE - CAP, s] + tail[SWAP_LANE - CAP, s + half]
-        sames = tail[SAME_LANE - CAP, s] + tail[SAME_LANE - CAP, s + half]
+        n = tail[COUNT_LANE - CAP, s]
+        care = tail[SAME_LANE - CAP, s]
 
         def add_rows(lo, hi, batch):
             items = [(range(j, min(j + batch, hi)), x, g) for j in range(lo, hi, batch) for x, g in pair]
@@ -356,15 +363,15 @@
                 def _():
                     add_rows(lo, min(lo + NEXT, ROWS - 1), batch)
 
-        @pl.when(swaps + sames == 0)
+        @pl.when(care == 0)
         def _():
             add_message(BATCH)
 
-        @pl.when((swaps == 0) & (sames > 0))
+        @pl.when(care == 1)
         def _():
             add_message(1)
 
-        @pl.when(swaps > 0)
+        @pl.when(care > 1)
         def _():
             for x, g in pair:
                 for j in range(ROWS - 1):
@@ -514,8 +521,9 @@
     return (1.0 - one_lon) * (1.0 - one_lon) * ((1.0 - one_lat) / (1.0 + one_lat))
 
 
-def smooth_kernel(grid, lon_len, local, done, ramp, carry):
-    done[0] = 1
+def smooth_kernel(grid, lon_len, lat_len, local, handed_on, ramp, carry):
+    for v in range(PROF):
+        handed_on[v // LEVQ, v % LEVQ] = lat_len[v // LEVQ, v % LEVQ]
     il = 1.0 / in_lanes(lon_len)
     fade = jnp.broadcast_to(jnp.exp(-il), (8, 128))
     stepno = (lax.broadcasted_iota(jnp.int32, (STEP, 128), 0) + 1).astype(jnp.float32)
@@ -576,16 +584,17 @@
     lax.fori_loop(0, STEP // 4, finish, 0)
 
 
-def smooth_band(grid, lon_len):
+def smooth_band(grid, lon_len, lat_len):
     return pl.pallas_call(
         smooth_kernel,
         grid=(TILES // SHARE,),
         out_shape=(
             jax.ShapeDtypeStruct((TILES * PLANE, 128), jnp.float32),
-            jax.ShapeDtypeStruct((1,), jnp.int32),
+            jax.ShapeDtypeStruct((F, LEVQ), jnp.float32),
         ),
         in_specs=[
             pl.BlockSpec((SHARE * PLANE, 128), lambda n: (n, 0)),
+            pl.BlockSpec(memory_space=pltpu.SMEM),
             pl.BlockSpec(memory_space=pltpu.SMEM),
         ],
         out_specs=(
@@ -599,10 +608,10 @@
         compiler_params=pltpu.CompilerParams(vmem_limit_bytes=VMEM_LIMIT),
         cost_estimate=pl.CostEstimate(flops=20_000_000, bytes_accessed=9_400_000, transcendentals=0),
         name="smooth_band",
-    )(grid, lon_len)
-
-
-def bands_kernel(ends, lat_len, _, out):
+    )(grid, lon_len, lat_len)
+
+
+def bands_kernel(ends, lat_len, out):
     im = 1.0 / in_lanes(lat_len)
     shape = ends.shape[1:]
     hop = jnp.broadcast_to(jnp.exp(-im * float(BAND)), shape)
@@ -620,16 +629,16 @@
         acc = hop * acc + ends[b]
 
 
-def join_bands(ends, lat_len, after):
+def join_bands(ends, lat_len):
     vmem = pl.BlockSpec(memory_space=pltpu.VMEM)
     return pl.pallas_call(
         bands_kernel,
         out_shape=jax.ShapeDtypeStruct(ends.shape, jnp.float32),
-        in_specs=[vmem] + [pl.BlockSpec(memory_space=pltpu.SMEM)] * 2,
+        in_specs=[vmem, pl.BlockSpec(memory_space=pltpu.SMEM)],
         out_specs=vmem,
         compiler_params=pltpu.CompilerParams(vmem_limit_bytes=8 * 1024 * 1024),
         name="join_bands",
-    )(ends, lat_len, after)
+    )(ends, lat_len)
 
 
 def turn_kernel(local, control, lon_len, lat_len, out, flipped):
@@ -809,8 +818,8 @@
 
     ends = ends.reshape(BANDS, -1, 128)
     ends = lax.all_to_all(ends, "lat", split_axis=0, concat_axis=0, tiled=True)
-    local, done = smooth_band(grid, len_lon)
-    joined = join_bands(ends, len_lat, done)
+    local, lengths = smooth_band(grid, len_lon, len_lat)
+    joined = join_bands(ends, lengths)
     joined = lax.all_to_all(joined, "lat", split_axis=0, concat_axis=0, tiled=True)
     parts = add_control(local, control, len_lon, len_lat)
     return add_bands(len_lat, len_lon, parts, joined.reshape(NLON // 2, 128))

time: 111 us -> 109 us (0.982)
  starting transfers between devices: 20.4 us -> 19.2 us
    all_to_all x1, starting transfers between devices: 5.03 us -> 3.8 us  [per_device(): ends = lax.all_to_all(ends, 'lat', split_axis=0, concat_axis=0, tiled=True)]
where the time goes in v5:
time: 109 us
  Pallas kernels  52 us (48%)
  waiting for transfers between devices  35.5 us (33%)
  starting transfers between devices  19.2 us (18%)
    all_to_all x1, waiting for transfers between devices, one_turn(): lax.all_to_all(messages, ('lat', 'lev'), split_axis=0, concat_axis=0, til...  30.6 us
    pallas_call x1, Pallas kernels, to_grid(): pl.pallas_call(grid_kernel, out_shape=(jax.ShapeDtypeStruct((NLON // 2, 1...  18.7 us
    all_to_all x1, starting transfers between devices, one_turn(): lax.all_to_all(messages, ('lat', 'lev'), split_axis=0, concat_axis=0, til...  11.5 us
    pallas_call x1, Pallas kernels, make_messages(): pl.pallas_call(send_kernel, out_shape=jax.ShapeDtypeStruct((BANDS, LEVS,...  11.1 us
    pallas_call x1, Pallas kernels, add_control(): pl.pallas_call(turn_kernel, grid=(NLON // 128 // WIDE,), out_shape=jax.Sh...  9.05 us
    pallas_call x1, Pallas kernels, smooth_band(): pl.pallas_call(smooth_kernel, grid=(TILES // SHARE,), out_shape=(jax.Shap...  6.61 us
    pallas_call x1, Pallas kernels, add_bands(): pl.pallas_call(last_kernel, out_shape=jax.ShapeDtypeStruct(parts.shape, j...  5.13 us
    all_to_all x1, starting transfers between devices, per_device(): lax.all_to_all(joined, 'lat', split_axis=0, concat_axis=0, tiled=True)  3.9 us
  transfers between devices with their start and end apart: 3, of which 3 were waited for; matrix products, arithmetic and copies ran while one was open for 0% of the time, Pallas kernels for 14%

profile of v5, /device:TPU:1, one launch (start us, length us, event | category | flops | bytes accessed | tf_op | source)
XLA Modules:
  0.0 108.5 jit_solution(9463607604616471472)
XLA Ops:
  0.0 0.0 copy-start.5
  0.0 0.0 copy-start.2
  0.0 0.0 copy-start.3
  0.0 0.0 copy-start.4
  0.0 11.1 %make_messages.2 = f32[32,4,32,128]{3,2,1,0:T(8,128)} custom-call(s32[1]{0:T(128)} %constant.4.clone.1.turn, f32[2048,128]{1,0:T(8,128)} %vals_in.1, s32[1,2048]{1,0:T(1,128)} %bitcast.21, s32[1,2048]{1,0:T(1,128)} %bitcast.23, f32[128,768]{1,0:T(8,128)} %bitcast.16, f32[4,768]{1,0:T(4,128)} %len_lev.1), custom_call_target="tpu_custom_call" | custom-call | tf_op jit(solution)/shard_map/make_messages/pallas_call | solution.py:255
  11.1 11.5 %all-to-all-start.1 = ((f32[128,32,128]{2,1,0:T(8,128)}), f32[128,32,128]{2,1,0:T(8,128)S(1)}, u32[]{:S(2)}, u32[]{:S(2)}) async-start(f32[128,32,128]{2,1,0:T(8,128)} %bitcast.19), calls=%async_computation.1 | async-start | bytes 4194304 | tf_op jit(solution)/shard_map/all_to_all | solution.py:803
  22.6 30.6 %all-to-all-done.1.recv = f32[128,32,128]{2,1,0:T(8,128)S(1)} async-done(((f32[128,32,128]{2,1,0:T(8,128)}), f32[128,32,128]{2,1,0:T(8,128)S(1)}, u32[]{:S(2)}, u32[]{:S(2)}) %all-to-all-start.1) | async-done | bytes 2097184 | tf_op jit(solution)/shard_map/all_to_all | solution.py:803
  53.2 0.0 copy-done.5
  53.2 18.7 %to_grid.2 = (f32[768,128]{1,0:T(8,128)}, f32[9216,128]{1,0:T(8,128)}, s32[1]{0:T(128)}) custom-call(f32[128,32,128]{2,1,0:T(8,128)S(1)} %all-to-all-done.1.recv, f32[4,8]{1,0:T(4,128)S(1)} %copy-done.5), custom_call_target="tpu_custom_call" | custom-call | tf_op jit(solution)/shard_map/to_grid/pallas_call | solution.py:467
  71.9 0.0 copy-done.2
  71.9 0.0 copy-done.3
  71.9 0.0 copy-done.4
  71.9 0.9 while.12
  72.8 3.8 %all-to-all-start.2 = ((f32[32,24,128]{2,1,0:T(8,128)}), f32[32,24,128]{2,1,0:T(8,128)S(1)}, u32[]{:S(2)}, u32[]{:S(2)}) async-start(f32[32,24,128]{2,1,0:T(8,128)} %bitcast.18), calls=%async_computation.2 | async-start | bytes 786432 | tf_op jit(solution)/shard_map/all_to_all | solution.py:820
  76.6 6.6 %smooth_band.1 = (f32[9216,128]{1,0:T(8,128)}, f32[4,8]{1,0:T(4,128)}) custom-call(f32[9216,128]{1,0:T(8,128)} %get-tuple-element.69.grid, f32[4,8]{1,0:T(4,128)} %lon_len.5, f32[4,8]{1,0:T(4,128)S(1)} %get-tuple-element.202), custom_call_target="tpu_custom_call" | custom-call | flops 20000000 | bytes 9400000 | tf_op jit(solution)/shard_map/smooth_band/pallas_call | solution.py:588
  83.2 3.7 %all-to-all-done.2.ends = f32[32,24,128]{2,1,0:T(8,128)S(1)} async-done(((f32[32,24,128]{2,1,0:T(8,128)}), f32[32,24,128]{2,1,0:T(8,128)S(1)}, u32[]{:S(2)}, u32[]{:S(2)}) %all-to-all-start.2) | async-done | bytes 393248 | tf_op jit(solution)/shard_map/all_to_all | solution.py:820
  86.9 0.0 copy-start.1
  86.9 0.7 copy-done.1
  87.5 1.5 %join_bands.1 = f32[32,24,128]{2,1,0:T(8,128)} custom-call(f32[32,24,128]{2,1,0:T(8,128)S(1)} %all-to-all-done.2.ends, f32[4,8]{1,0:T(4,128)S(1)} %copy-done.1), custom_call_target="tpu_custom_call" | custom-call | tf_op jit(solution)/shard_map/join_bands/pallas_call | solution.py:634
  89.1 3.9 %all-to-all-start.3 = ((f32[32,24,128]{2,1,0:T(8,128)}), f32[32,24,128]{2,1,0:T(8,128)S(1)}, u32[]{:S(2)}, u32[]{:S(2)}) async-start(f32[32,24,128]{2,1,0:T(8,128)} %join_bands.1), calls=%async_computation.3 | async-start | bytes 786432 | tf_op jit(solution)/shard_map/all_to_all | solution.py:823
  93.0 0.0 copy-start
  93.0 9.1 %add_control.1.parts = f32[4,8,24,1536]{3,2,1,0:T(8,128)} custom-call(f32[6,1536,128]{2,1,0:T(8,128)} %bitcast.20, f32[4,8,24,1536]{3,2,1,0:T(8,128)} %control.1, f32[4,8]{1,0:T(4,128)} %lon_len.5, f32[4,8]{1,0:T(4,128)S(1)} %get-tuple-element.202), custom_call_target="tpu_custom_call" | custom-call | flops 20000000 | bytes 15000000 | tf_op jit(solution)/shard_map/add_control/pallas_call | solution.py:679
  102.0 1.2 %all-to-all-done.3 = f32[32,24,128]{2,1,0:T(8,128)S(1)} async-done(((f32[32,24,128]{2,1,0:T(8,128)}), f32[32,24,128]{2,1,0:T(8,128)S(1)}, u32[]{:S(2)}, u32[]{:S(2)}) %all-to-all-start.3) | async-done | bytes 393248 | tf_op jit(solution)/shard_map/all_to_all | solution.py:823
  103.2 0.0 copy-done
  103.3 5.1 %add_bands.1 = f32[4,8,24,1536]{3,2,1,0:T(8,128)} custom-call(f32[4,8]{1,0:T(4,128)S(1)} %get-tuple-element.202, f32[4,8]{1,0:T(4,128)S(1)} %copy-done, f32[4,8,24,1536]{3,2,1,0:T(8,128)} %add_control.1.parts, f32[768,128]{1,0:T(8,128)S(1)} %bitcast.14), custom_call_target="tpu_custom_call", output_to_operand_aliasing={{}: (2, {})} | custom-call | tf_op jit(solution)/shard_map/add_bands/pallas_call | solution.py:776
Async XLA Ops:
  0.0 53.2 %copy-start.5 = (f32[4,8]{1,0:T(4,128)S(1)}, f32[4,8]{1,0:T(4,128)}, u32[]{:S(2)}) copy-start(f32[4,8]{1,0:T(4,128)} %lat_len.7) | copy-start | bytes 388
  0.0 71.9 %copy-start.2 = (f32[2048,128]{1,0:T(8,128)S(1)}, f32[2048,128]{1,0:T(8,128)}, u32[]{:S(2)}) copy-start(f32[2048,128]{1,0:T(8,128)} %vals_in.1) | copy-start | bytes 3145732
  0.0 71.9 %copy-start.3 = (f32[4,32,768]{2,1,0:T(8,128)S(1)}, f32[4,32,768]{2,1,0:T(8,128)}, u32[]{:S(2)}) copy-start(f32[4,32,768]{2,1,0:T(8,128)} %param.14) | copy-start | bytes 1179652
  0.0 71.9 %copy-start.4 = (f32[4,768]{1,0:T(4,128)S(1)}, f32[4,768]{1,0:T(4,128)}, u32[]{:S(2)}) copy-start(f32[4,768]{1,0:T(4,128)} %len_lev.1) | copy-start | bytes 36868
  11.1 42.1 %all-to-all-start.1 = ((f32[128,32,128]{2,1,0:T(8,128)}), f32[128,32,128]{2,1,0:T(8,128)S(1)}, u32[]{:S(2)}, u32[]{:S(2)}) async-start(f32[128,32,128]{2,1,0:T(8,128)} %bitcast.19), calls=%async_computation.1 | async-start | bytes 4194304 | tf_op jit(solution)/shard_map/all_to_all | solution.py:803
  72.8 14.1 %all-to-all-start.2 = ((f32[32,24,128]{2,1,0:T(8,128)}), f32[32,24,128]{2,1,0:T(8,128)S(1)}, u32[]{:S(2)}, u32[]{:S(2)}) async-start(f32[32,24,128]{2,1,0:T(8,128)} %bitcast.18), calls=%async_computation.2 | async-start | bytes 786432 | tf_op jit(solution)/shard_map/all_to_all | solution.py:820
  86.9 0.7 copy-start.1
  89.1 14.2 %all-to-all-start.3 = ((f32[32,24,128]{2,1,0:T(8,128)}), f32[32,24,128]{2,1,0:T(8,128)S(1)}, u32[]{:S(2)}, u32[]{:S(2)}) async-start(f32[32,24,128]{2,1,0:T(8,128)} %join_bands.1), calls=%async_computation.3 | async-start | bytes 786432 | tf_op jit(solution)/shard_map/all_to_all | solution.py:823
  93.0 10.3 %copy-start = (f32[4,8]{1,0:T(4,128)S(1)}, f32[4,8]{1,0:T(4,128)}, u32[]{:S(2)}) copy-start(f32[4,8]{1,0:T(4,128)} %lon_len.5) | copy-start | bytes 388

commit v6 on v5

--- a/solution.py
+++ b/solution.py
@@ -33,7 +33,7 @@
 BATCH = 3
 SHARE = 2
 WIDE = 4
-UNROLL = 16
+UNROLL = 32
 FIRST, NEXT = 18, 6
 PARTS = 3
 PAIRS = BAND // 2
@@ -696,8 +696,8 @@
 
 def last_kernel(lat_len, lon_len, parts, joined, out, held, from_start, from_end, ys, south, north, sem):
     half = STEP // 2
-    per = LEVQ // 4
-    chunks = [(k // 4, pl.ds(k % 4 * per, per)) for k in range(F * 4)]
+    per = LEVQ // 2
+    chunks = [(k // 2, pl.ds(k % 2 * per, per)) for k in range(F * 2)]
     fetches = [pltpu.make_async_copy(parts.at[c], held.at[c], sem.at[0, k]) for k, c in enumerate(chunks)]
     stores = [pltpu.make_async_copy(held.at[c], out.at[c], sem.at[1, k]) for k, c in enumerate(chunks)]
     for copy in fetches:
@@ -785,7 +785,7 @@
             pltpu.VMEM((NLON // 2, 128), jnp.float32),
             pltpu.VMEM((NLON // 128, PROF, 128), jnp.float32),
             pltpu.VMEM((NLON // 128, PROF, 128), jnp.float32),
-            pltpu.SemaphoreType.DMA((2, F * 4)),
+            pltpu.SemaphoreType.DMA((2, F * 2)),
         ],
         compiler_params=pltpu.CompilerParams(vmem_limit_bytes=24 * 1024 * 1024),
         input_output_aliases={2: 0},

time: 109 us -> 108 us (level)
  transfers between devices with their start and end apart: 3 -> 3, of which waited for: 3 -> 3; matrix products, arithmetic and copies ran while one was open for 0% -> 0% of each run, Pallas kernels for 14% -> 15%
where the time goes in v6:
time: 108 us
  Pallas kernels  51 us (47%)
  waiting for transfers between devices  35.3 us (33%)
  starting transfers between devices  19.4 us (18%)
    all_to_all x1, waiting for transfers between devices, one_turn(): lax.all_to_all(messages, ('lat', 'lev'), split_axis=0, concat_axis=0, til...  30.6 us
    pallas_call x1, Pallas kernels, to_grid(): pl.pallas_call(grid_kernel, out_shape=(jax.ShapeDtypeStruct((NLON // 2, 1...  18 us
    all_to_all x1, starting transfers between devices, one_turn(): lax.all_to_all(messages, ('lat', 'lev'), split_axis=0, concat_axis=0, til...  11.5 us
    pallas_call x1, Pallas kernels, make_messages(): pl.pallas_call(send_kernel, out_shape=jax.ShapeDtypeStruct((BANDS, LEVS,...  11.1 us
    pallas_call x1, Pallas kernels, add_control(): pl.pallas_call(turn_kernel, grid=(NLON // 128 // WIDE,), out_shape=jax.Sh...  9.05 us
    pallas_call x1, Pallas kernels, smooth_band(): pl.pallas_call(smooth_kernel, grid=(TILES // SHARE,), out_shape=(jax.Shap...  6.61 us
    pallas_call x1, Pallas kernels, add_bands(): pl.pallas_call(last_kernel, out_shape=jax.ShapeDtypeStruct(parts.shape, j...  4.68 us
    all_to_all x1, starting transfers between devices, per_device(): ends = lax.all_to_all(ends, 'lat', split_axis=0, concat_axis=0, tiled=True)  3.98 us
  transfers between devices with their start and end apart: 3, of which 3 were waited for; matrix products, arithmetic and copies ran while one was open for 0% of the time, Pallas kernels for 15%

profile of v6, /device:TPU:1, one launch (start us, length us, event | category | flops | bytes accessed | tf_op | source)
XLA Modules:
  0.0 107.5 jit_solution(5257556288012055763)
XLA Ops:
  0.0 0.0 copy-start.5
  0.0 0.0 copy-start.2
  0.0 0.0 copy-start.3
  0.0 0.0 copy-start.4
  0.0 11.1 %make_messages.2 = f32[32,4,32,128]{3,2,1,0:T(8,128)} custom-call(s32[1]{0:T(128)} %constant.4.clone.1.turn, f32[2048,128]{1,0:T(8,128)} %vals_in.1, s32[1,2048]{1,0:T(1,128)} %bitcast.21, s32[1,2048]{1,0:T(1,128)} %bitcast.23, f32[128,768]{1,0:T(8,128)} %bitcast.16, f32[4,768]{1,0:T(4,128)} %len_lev.1), custom_call_target="tpu_custom_call" | custom-call | tf_op jit(solution)/shard_map/make_messages/pallas_call | solution.py:255
  11.1 11.5 %all-to-all-start.1 = ((f32[128,32,128]{2,1,0:T(8,128)}), f32[128,32,128]{2,1,0:T(8,128)S(1)}, u32[]{:S(2)}, u32[]{:S(2)}) async-start(f32[128,32,128]{2,1,0:T(8,128)} %bitcast.19), calls=%async_computation.1 | async-start | bytes 4194304 | tf_op jit(solution)/shard_map/all_to_all | solution.py:803
  22.6 30.6 %all-to-all-done.1.recv = f32[128,32,128]{2,1,0:T(8,128)S(1)} async-done(((f32[128,32,128]{2,1,0:T(8,128)}), f32[128,32,128]{2,1,0:T(8,128)S(1)}, u32[]{:S(2)}, u32[]{:S(2)}) %all-to-all-start.1) | async-done | bytes 2097184 | tf_op jit(solution)/shard_map/all_to_all | solution.py:803
  53.2 0.0 copy-done.5
  53.2 18.0 %to_grid.2 = (f32[768,128]{1,0:T(8,128)}, f32[9216,128]{1,0:T(8,128)}, s32[1]{0:T(128)}) custom-call(f32[128,32,128]{2,1,0:T(8,128)S(1)} %all-to-all-done.1.recv, f32[4,8]{1,0:T(4,128)S(1)} %copy-done.5), custom_call_target="tpu_custom_call" | custom-call | tf_op jit(solution)/shard_map/to_grid/pallas_call | solution.py:467
  71.2 0.0 copy-done.2
  71.2 0.0 copy-done.3
  71.2 0.0 copy-done.4
  71.2 0.9 while.12
  72.1 4.0 %all-to-all-start.2 = ((f32[32,24,128]{2,1,0:T(8,128)}), f32[32,24,128]{2,1,0:T(8,128)S(1)}, u32[]{:S(2)}, u32[]{:S(2)}) async-start(f32[32,24,128]{2,1,0:T(8,128)} %bitcast.18), calls=%async_computation.2 | async-start | bytes 786432 | tf_op jit(solution)/shard_map/all_to_all | solution.py:820
  76.1 6.6 %smooth_band.1 = (f32[9216,128]{1,0:T(8,128)}, f32[4,8]{1,0:T(4,128)}) custom-call(f32[9216,128]{1,0:T(8,128)} %get-tuple-element.69.grid, f32[4,8]{1,0:T(4,128)} %lon_len.5, f32[4,8]{1,0:T(4,128)S(1)} %get-tuple-element.202), custom_call_target="tpu_custom_call" | custom-call | flops 20000000 | bytes 9400000 | tf_op jit(solution)/shard_map/smooth_band/pallas_call | solution.py:588
  82.7 3.6 %all-to-all-done.2.ends = f32[32,24,128]{2,1,0:T(8,128)S(1)} async-done(((f32[32,24,128]{2,1,0:T(8,128)}), f32[32,24,128]{2,1,0:T(8,128)S(1)}, u32[]{:S(2)}, u32[]{:S(2)}) %all-to-all-start.2) | async-done | bytes 393248 | tf_op jit(solution)/shard_map/all_to_all | solution.py:820
  86.3 0.0 copy-start.1
  86.3 0.7 copy-done.1
  87.0 1.5 %join_bands.1 = f32[32,24,128]{2,1,0:T(8,128)} custom-call(f32[32,24,128]{2,1,0:T(8,128)S(1)} %all-to-all-done.2.ends, f32[4,8]{1,0:T(4,128)S(1)} %copy-done.1), custom_call_target="tpu_custom_call" | custom-call | tf_op jit(solution)/shard_map/join_bands/pallas_call | solution.py:634
  88.5 3.9 %all-to-all-start.3 = ((f32[32,24,128]{2,1,0:T(8,128)}), f32[32,24,128]{2,1,0:T(8,128)S(1)}, u32[]{:S(2)}, u32[]{:S(2)}) async-start(f32[32,24,128]{2,1,0:T(8,128)} %join_bands.1), calls=%async_computation.3 | async-start | bytes 786432 | tf_op jit(solution)/shard_map/all_to_all | solution.py:823
  92.4 0.0 copy-start
  92.4 9.1 %add_control.1.parts = f32[4,8,24,1536]{3,2,1,0:T(8,128)} custom-call(f32[6,1536,128]{2,1,0:T(8,128)} %bitcast.20, f32[4,8,24,1536]{3,2,1,0:T(8,128)} %control.1, f32[4,8]{1,0:T(4,128)} %lon_len.5, f32[4,8]{1,0:T(4,128)S(1)} %get-tuple-element.202), custom_call_target="tpu_custom_call" | custom-call | flops 20000000 | bytes 15000000 | tf_op jit(solution)/shard_map/add_control/pallas_call | solution.py:679
  101.5 1.2 %all-to-all-done.3 = f32[32,24,128]{2,1,0:T(8,128)S(1)} async-done(((f32[32,24,128]{2,1,0:T(8,128)}), f32[32,24,128]{2,1,0:T(8,128)S(1)}, u32[]{:S(2)}, u32[]{:S(2)}) %all-to-all-start.3) | async-done | bytes 393248 | tf_op jit(solution)/shard_map/all_to_all | solution.py:823
  102.7 0.0 copy-done
  102.7 4.7 %add_bands.1 = f32[4,8,24,1536]{3,2,1,0:T(8,128)} custom-call(f32[4,8]{1,0:T(4,128)S(1)} %get-tuple-element.202, f32[4,8]{1,0:T(4,128)S(1)} %copy-done, f32[4,8,24,1536]{3,2,1,0:T(8,128)} %add_control.1.parts, f32[768,128]{1,0:T(8,128)S(1)} %bitcast.14), custom_call_target="tpu_custom_call", output_to_operand_aliasing={{}: (2, {})} | custom-call | tf_op jit(solution)/shard_map/add_bands/pallas_call | solution.py:776
Async XLA Ops:
  0.0 53.2 %copy-start.5 = (f32[4,8]{1,0:T(4,128)S(1)}, f32[4,8]{1,0:T(4,128)}, u32[]{:S(2)}) copy-start(f32[4,8]{1,0:T(4,128)} %lat_len.7) | copy-start | bytes 388
  0.0 71.2 %copy-start.2 = (f32[2048,128]{1,0:T(8,128)S(1)}, f32[2048,128]{1,0:T(8,128)}, u32[]{:S(2)}) copy-start(f32[2048,128]{1,0:T(8,128)} %vals_in.1) | copy-start | bytes 3145732
  0.0 71.2 %copy-start.3 = (f32[4,32,768]{2,1,0:T(8,128)S(1)}, f32[4,32,768]{2,1,0:T(8,128)}, u32[]{:S(2)}) copy-start(f32[4,32,768]{2,1,0:T(8,128)} %param.14) | copy-start | bytes 1179652
  0.0 71.2 %copy-start.4 = (f32[4,768]{1,0:T(4,128)S(1)}, f32[4,768]{1,0:T(4,128)}, u32[]{:S(2)}) copy-start(f32[4,768]{1,0:T(4,128)} %len_lev.1) | copy-start | bytes 36868
  11.1 42.1 %all-to-all-start.1 = ((f32[128,32,128]{2,1,0:T(8,128)}), f32[128,32,128]{2,1,0:T(8,128)S(1)}, u32[]{:S(2)}, u32[]{:S(2)}) async-start(f32[128,32,128]{2,1,0:T(8,128)} %bitcast.19), calls=%async_computation.1 | async-start | bytes 4194304 | tf_op jit(solution)/shard_map/all_to_all | solution.py:803
  72.1 14.2 %all-to-all-start.2 = ((f32[32,24,128]{2,1,0:T(8,128)}), f32[32,24,128]{2,1,0:T(8,128)S(1)}, u32[]{:S(2)}, u32[]{:S(2)}) async-start(f32[32,24,128]{2,1,0:T(8,128)} %bitcast.18), calls=%async_computation.2 | async-start | bytes 786432 | tf_op jit(solution)/shard_map/all_to_all | solution.py:820
  86.3 0.7 copy-start.1
  88.5 14.2 %all-to-all-start.3 = ((f32[32,24,128]{2,1,0:T(8,128)}), f32[32,24,128]{2,1,0:T(8,128)S(1)}, u32[]{:S(2)}, u32[]{:S(2)}) async-start(f32[32,24,128]{2,1,0:T(8,128)} %join_bands.1), calls=%async_computation.3 | async-start | bytes 786432 | tf_op jit(solution)/shard_map/all_to_all | solution.py:823
  92.4 10.3 %copy-start = (f32[4,8]{1,0:T(4,128)S(1)}, f32[4,8]{1,0:T(4,128)}, u32[]{:S(2)}) copy-start(f32[4,8]{1,0:T(4,128)} %lon_len.5) | copy-start | bytes 388
